TPU v7x, 256 devices: a whole 4x4x8 slice. The times are simulated.
256 devices in a mesh: seq: 32 (over y, x, core), exp: 8 (over z).
Axes of the slice: x: 4, y: 4, z: 8, core: 2. Of those that a mesh axis runs over, the one named last changes fastest.
Arguments:
- mixer_input: bfloat16 [32768, 8192], P('seq', 'exp'), may hold values from -6 to 6
- log_decay: float32 [128, 32768], P('exp', 'seq'), may hold values from -1 to 0, as said below
- b_rows: bfloat16 [32768, 128], P('seq'), may hold values from -0.23925781 to 0.23925781
- c_rows: bfloat16 [32768, 128], P('seq'), may hold values from -0.23925781 to 0.23925781
- skip_gain: float32 [128], P('exp'), may hold values from 0.5 to 1.5
- grad_out: bfloat16 [32768, 8192], P('seq', 'exp'), may hold values from -6 to 6
Outputs:
- mixer_out: bfloat16 [32768, 8192], P('seq', 'exp')
- grad_input: bfloat16 [32768, 8192], P('seq', 'exp')
- grad_log_decay: float32 [128, 32768], P('exp', 'seq')
- grad_b: float32 [32768, 128], P(('seq', 'exp'))
- grad_c: float32 [32768, 128], P(('seq', 'exp'))
Inputs may be any that keep to these rules, and one draw needn't show every extreme that they name: log_decay is negative everywhere.
All inputs are finite; a program needn't handle non-finite values.
Results may differ from a plain program's by a relative error of at most 0.02.
Values sent between devices are 32-bit elements; how exact they have to be, the bound alone decides.
A program may use at most 192 MiB of HBM per device.

v0:
```python
import jax
import jax.numpy as jnp
from jax import lax
from jax.sharding import PartitionSpec as P

SPAN = 256


def entering_2(part, axis, combine, identity, reverse):
    count = lax.axis_size(axis)
    place = lax.axis_index(axis)
    ahead = count - 1 - place if reverse else place
    gathered = jax.tree.map(lambda a: lax.all_gather(a, axis), part)
    state = jax.tree.map(lambda a, e: jnp.zeros_like(a) + jnp.asarray(e, a.dtype), part, identity)

    def one(hop, state):
        source = count - 1 - hop if reverse else hop
        return combine(
            state, jax.tree.map(lambda a: lax.dynamic_index_in_dim(a, source, 0, False), gathered)
        )

    return lax.fori_loop(0, ahead, one, state)


def lowp(value):
    return value.astype(jnp.bfloat16)


def mixer_blocks(inputs_x, log_rates, b_in, c_in, skip_part, entering):
    length, channels = inputs_x.shape
    head_count = log_rates.shape[0]
    head_size = channels // head_count
    state_size = b_in.shape[1]
    block_count = length // SPAN
    split_x = inputs_x.reshape(block_count, SPAN, head_count, head_size)
    split_rates = log_rates.reshape(head_count, block_count, SPAN).transpose(1, 0, 2)
    split_b = b_in.reshape(block_count, SPAN, state_size)
    split_c = c_in.reshape(block_count, SPAN, state_size)
    causal = jnp.arange(SPAN)[:, None] >= jnp.arange(SPAN)[None, :]

    def advance(running, pieces):
        piece_x, piece_rates, piece_b, piece_c = pieces
        cumul = jnp.cumsum(piece_rates, axis=1)
        spread = jnp.where(causal[None], cumul[:, :, None] - cumul[:, None, :], -jnp.inf)
        match_cb = jnp.dot(lowp(piece_c), lowp(piece_b).T, preferred_element_type=jnp.float32)
        weights_ts = jnp.exp(spread) * match_cb[None]
        inner_y = jnp.einsum(
            "hts,shp->thp", lowp(weights_ts), lowp(piece_x), preferred_element_type=jnp.float32
        )
        from_state = jnp.einsum(
            "tn,hnp->thp", lowp(piece_c), lowp(running), preferred_element_type=jnp.float32
        )
        from_state = from_state * jnp.exp(cumul).T[:, :, None]
        tail_weight = jnp.exp(cumul[:, -1:] - cumul)
        scaled_x = piece_x * tail_weight.T[:, :, None]
        fresh = jnp.einsum(
            "sn,shp->hnp", lowp(piece_b), lowp(scaled_x), preferred_element_type=jnp.float32
        )
        updated = jnp.exp(cumul[:, -1])[:, None, None] * running + fresh
        output_y = inner_y + from_state + skip_part[None, :, None] * piece_x
        return (updated, output_y)

    final, outputs = lax.scan(advance, entering, (split_x, split_rates, split_b, split_c))
    return (outputs.reshape(length, channels), final)


def scan_join(former, latter):
    return (former[0] + latter[0], jnp.exp(latter[0])[:, None, None] * former[1] + latter[1])


def body(mixer_input, log_decay, b_rows, c_rows, skip_gain, grad_out):
    x_full = mixer_input.astype(jnp.float32)
    b_full = b_rows.astype(jnp.float32)
    c_full = c_rows.astype(jnp.float32)
    grad_full = grad_out.astype(jnp.float32)
    head_count = log_decay.shape[0]
    length = x_full.shape[0]
    head_size = x_full.shape[1] // head_count
    cumul = jnp.cumsum(log_decay, axis=1)
    totals = cumul[:, -1]
    tail_weight = jnp.exp(totals[:, None] - cumul)
    shaped_x = mixer_input.reshape(length, head_count, head_size)
    shaped_grad = grad_out.reshape(length, head_count, head_size)
    state_term = jnp.einsum(
        "sn,shp->hnp",
        b_rows,
        lowp(shaped_x * tail_weight.T[:, :, None]),
        preferred_element_type=jnp.float32,
    )
    grad_term = jnp.einsum(
        "tn,thp->hnp",
        c_rows,
        lowp(shaped_grad * jnp.exp(cumul).T[:, :, None]),
        preferred_element_type=jnp.float32,
    )
    zero_state = jnp.zeros_like(state_term)
    zero_log = jnp.zeros_like(totals)
    forward_pair = entering_2((totals, state_term), "seq", scan_join, (zero_log, zero_state), False)
    backward_pair = entering_2((totals, grad_term), "seq", scan_join, (zero_log, zero_state), True)
    carried = forward_pair[1]
    incoming = backward_pair[1]

    def forward_map(part_x, part_rates, part_b, part_c, entering):
        return mixer_blocks(part_x, part_rates, part_b, part_c, skip_gain, entering)

    primal_out, pullback = jax.vjp(forward_map, x_full, log_decay, b_full, c_full, carried)
    grads = pullback((grad_full, incoming))
    summed_b, summed_c = (
        lax.psum_scatter(grads[2], "exp", scatter_dimension=0, tiled=True),
        lax.psum_scatter(grads[3], "exp", scatter_dimension=0, tiled=True),
    )
    return (
        primal_out[0].astype(jnp.bfloat16),
        grads[0].astype(jnp.bfloat16),
        grads[1],
        summed_b,
        summed_c,
    )


def solution(mesh):
    return jax.shard_map(
        body,
        mesh=mesh,
        in_specs=(
            P("seq", "exp"),
            P("exp", "seq"),
            P("seq", None),
            P("seq", None),
            P("exp"),
            P("seq", "exp"),
        ),
        out_specs=(
            P("seq", "exp"),
            P("seq", "exp"),
            P("exp", "seq"),
            P(("seq", "exp"), None),
            P(("seq", "exp"), None),
        ),
        check_vma=False,
    )
```

profile of v0, /device:TPU:8, one launch (start us, length us, event | category | flops | bytes accessed | tf_op | source)
XLA Modules:
  0.0 424.5 jit_solution(6181207173458748384)
XLA Ops:
  8.1 4.5 %reduce-window.48 = f32[16,8,128]{2,1,0:T(8,128)S(1)} reduce-window(f32[16,8,128]{2,1,0:T(8,128)S(1)} %bitcast.593, f32[]{:T(128)} %constant.221.clone.1), window={size=1x1x128 pad=0_0x0_0x127_0}, to_apply=%region_0.0 | reduce-window | flops 2080768 | bytes 131076 | tf_op jit(solution)/shard_map/reduce-window.2
  13.3 2.9 copy.126
  18.9 2.9 copy.132
  24.4 5.0 %reshape.454 = f32[4,256,16,64]{1,0,3,2:T(4,128)} reshape(bf16[1024,1024]{0,1:T(8,128)(2,1)} %copy-done.1) | data formatting | bytes 6291456 | tf_op jit(solution)/shard_map/jvp()/reshape | solution.py:35
  29.5 3.4 reshape.461
  34.3 56.2 %all-reduce.2 = f32[512]{0:T(512)S(1)} all-reduce(f32[512]{0:T(512)S(1)} %bitcast_dynamic-update-slice_fusion.6), channel_id=2, replica_groups=mesh['seq'=32,'exp'=8] {'seq'}, use_global_device_ids=true, to_apply=%add.2 | all-reduce | flops 512 | bytes 4096
  90.6 5.0 %copy.130 = f32[4,256,16,64]{1,3,2,0:T(8,128)} copy(f32[4,256,16,64]{1,0,3,2:T(4,128)} %reshape.454) | data formatting | bytes 8388608
  99.5 13.6 %while.105 = (s32[]{:T(128)}, f32[16,128,64]{2,1,0:T(8,128)S(1)}, s32[]{:T(128)}, f32[32,16]{1,0:T(8,128)S(1)}, f32[32,16,128,64]{2,3,1,0:T(8,128)}) while((s32[]{:T(128)}, f32[16,128,64]{2,1,0:T(8,128)S(1)}, s32[]{:T(128)}, f32[32,16]{1,0:T(8,128)S(1)}, f32[32,16,128,64]{2,3,1,0:T(8,128)}) %tuple.228), condition=%wide.region_3.4_spmd.clone, body=%wide.region_2.3_spmd.sunk.clone | while | flops 262149 | bytes 3670311 | solution.py:22
  113.5 67.8 %while.108 = (s32[]{:T(128)}, f32[16,128,64]{1,2,0:T(8,128)S(1)}, bf16[4,256,16,64]{1,3,2,0:T(8,128)(2,1)}, bf16[4,128,256]{1,2,0:T(8,128)(2,1)}, bf16[4,256,128...) while((s32[]{:T(128)}, f32[16,128,64]{1,2,0:T(8,128)S(1)}, ...), condition=%wide.region_7.8_spmd.clone.clone.clone, body=%wide.region_4.7_spmd.clone.clone.sunk.clone | while | flops 298999872 | bytes 40053748 | solution.py:63
  182.0 39.3 %while.106 = (s32[]{:T(128)}, f32[16,128,64]{2,1,0:T(8,128)S(1)}, s32[]{:T(128)}, f32[32,16]{1,0:T(8,128)S(1)}, f32[32,16,128,64]{2,3,1,0:T(8,128)}) while((s32[]{:T(128)}, f32[16,128,64]{2,1,0:T(8,128)S(1)}, s32[]{:T(128)}, f32[32,16]{1,0:T(8,128)S(1)}, f32[32,16,128,64]{2,3,1,0:T(8,128)}) %tuple.232), condition=%wide.region_9.10_spmd.clone, body=%wide.region_8.9_spmd.sunk.clone | while | flops 262150 | bytes 3670323 | solution.py:22
  223.2 109.3 %while.107 = (s32[]{:T(128)}, f32[16,128,64]{1,2,0:T(8,128)S(1)}, bf16[4,256,16,64]{1,3,2,0:T(8,128)(2,1)}, f32[4,16,256]{2,1,0:T(8,128)S(1)}, f32[4,256,128]{2,...) while((s32[]{:T(128)}, f32[16,128,64]{1,2,0:T(8,128)S(1)}, ...), condition=%wide.region_20.21_spmd.clone.clone, body=%wide.region_10.20_spmd.clone.sunk.clone | while | flops 583987264 | bytes 26419276 | solution.py:63
  223.2 3.3 constant_dynamic-slice_fusion.20
  227.5 4.1 fusion.242
  237.9 2.5 reduce-window.64
  241.5 2.9 fusion.241
  250.6 3.3 constant_dynamic-slice_fusion.20
  254.8 4.1 fusion.242
  265.3 2.5 reduce-window.64
  268.8 2.9 fusion.241
  277.9 3.3 constant_dynamic-slice_fusion.20
  282.1 4.1 fusion.242
  292.6 2.5 reduce-window.64
  296.1 2.9 fusion.241
  305.2 3.3 constant_dynamic-slice_fusion.20
  309.5 4.1 fusion.242
  323.4 2.8 fusion.241
  333.1 6.2 %copy.145 = bf16[4,256,16,64]{3,2,1,0:T(8,128)(2,1)} copy(bf16[4,256,16,64]{1,3,2,0:T(8,128)(2,1)} %get-tuple-element.1033) | data formatting | bytes 4194304
  339.3 6.6 %reshape.487 = bf16[1024,1024]{1,0:T(8,128)(2,1)} reshape(bf16[4,256,16,64]{3,2,1,0:T(8,128)(2,1)} %copy.145) | data formatting | bytes 4194304
  346.6 4.8 %copy.144 = bf16[4,256,16,64]{3,2,1,0:T(8,128)(2,1)} copy(bf16[4,256,16,64]{1,3,2,0:T(8,128)(2,1)S(1)} %copy-done.3) | data formatting | bytes 4194304
  351.4 6.5 %reshape.486 = bf16[1024,1024]{1,0:T(8,128)(2,1)} reshape(bf16[4,256,16,64]{3,2,1,0:T(8,128)(2,1)} %copy.144) | data formatting | bytes 4194304
  357.9 21.1 %reduce-scatter.3.cloned.1.call-done = f32[128,128]{1,0:T(8,128)} async-done(((f32[1024,128]{1,0:T(8,128)}), f32[128,128]{1,0:T(8,128)}) %reduce-scatter.3.cloned.1.call-update) | async-done | bytes 65552 | tf_op jit(solution)/shard_map/reduce_scatter | solution.py:109
  379.0 39.0 %reduce-scatter.5.cloned.1.call-done = f32[128,128]{1,0:T(8,128)} async-done(((f32[1024,128]{1,0:T(8,128)}), f32[128,128]{1,0:T(8,128)}) %reduce-scatter.5.cloned.1.call-update) | async-done | bytes 65552 | tf_op jit(solution)/shard_map/reduce_scatter | solution.py:110
  (457 shorter events, 194.9 us)
Async XLA Ops:
  7.2 92.3 %all-gather.6.cloned.1.call-start = ((), (), s32[]{:S(2)}) async-start(), calls=%async_computation.4 | async-start | bytes 17301504 | tf_op jit(solution)/shard_map/all_gather | solution.py:13
  16.1 2.7 copy-start.1
  16.2 1.1 copy-start.4
  18.9 162.4 %all-gather.8.cloned.1.call-start = ((), (), s32[]{:S(2)}) async-start(), calls=%async_computation.5 | async-start | bytes 17301504 | tf_op jit(solution)/shard_map/all_gather | solution.py:13
  21.8 1.0 copy-start.5
  24.3 5.2 %copy-start.8 = (f32[16,1024]{1,0:T(8,128)S(1)}, f32[16,1024]{1,0:T(8,128)}, u32[]{:S(2)}) copy-start(f32[16,1024]{1,0:T(8,128)} %param.15) | copy-start | bytes 196612
  24.3 354.7 %reduce-scatter.3.cloned.1.call-start = ((), (), s32[]{:S(2)}) async-start(), calls=%async_computation.2 | async-start | bytes 589824 | tf_op jit(solution)/shard_map/reduce_scatter | solution.py:109
  29.4 3.6 copy-start.11
  95.8 1.4 copy-start.2
  113.5 5.7 %copy-start.9 = (f32[1,16,1]{1,2,0:T(1,128)S(1)}, f32[1,16,1]{1,2,0:T(1,128)}, u32[]{:S(2)}) copy-start(f32[1,16,1]{1,2,0:T(1,128)} %get-tuple-element.2400) | copy-start | bytes 196 | tf_op jit(solution)/shard_map/jvp()/while
  115.9 3.4 copy-start
  130.5 5.7 %copy-start.9 = (f32[1,16,1]{1,2,0:T(1,128)S(1)}, f32[1,16,1]{1,2,0:T(1,128)}, u32[]{:S(2)}) copy-start(f32[1,16,1]{1,2,0:T(1,128)} %get-tuple-element.2400) | copy-start | bytes 196 | tf_op jit(solution)/shard_map/jvp()/while
  132.8 3.4 copy-start
  147.5 5.8 %copy-start.9 = (f32[1,16,1]{1,2,0:T(1,128)S(1)}, f32[1,16,1]{1,2,0:T(1,128)}, u32[]{:S(2)}) copy-start(f32[1,16,1]{1,2,0:T(1,128)} %get-tuple-element.2400) | copy-start | bytes 196 | tf_op jit(solution)/shard_map/jvp()/while
  149.9 3.4 copy-start
  164.4 5.8 %copy-start.9 = (f32[1,16,1]{1,2,0:T(1,128)S(1)}, f32[1,16,1]{1,2,0:T(1,128)}, u32[]{:S(2)}) copy-start(f32[1,16,1]{1,2,0:T(1,128)} %get-tuple-element.2400) | copy-start | bytes 196 | tf_op jit(solution)/shard_map/jvp()/while
  166.8 3.4 copy-start
  181.3 0.6 copy-start.6
  181.3 0.6 copy-start.7
  231.6 9.9 %copy-start.10 = (f32[1,16,1]{1,2,0:T(1,128)S(1)}, f32[1,16,1]{1,2,0:T(1,128)}, u32[]{:S(2)}) copy-start(f32[1,16,1]{1,2,0:T(1,128)} %get-tuple-element.2481) | copy-start | bytes 196 | tf_op jit(solution)/shard_map/transpose(jvp())/while
  258.9 9.9 %copy-start.10 = (f32[1,16,1]{1,2,0:T(1,128)S(1)}, f32[1,16,1]{1,2,0:T(1,128)}, u32[]{:S(2)}) copy-start(f32[1,16,1]{1,2,0:T(1,128)} %get-tuple-element.2481) | copy-start | bytes 196 | tf_op jit(solution)/shard_map/transpose(jvp())/while
  286.2 9.9 %copy-start.10 = (f32[1,16,1]{1,2,0:T(1,128)S(1)}, f32[1,16,1]{1,2,0:T(1,128)}, u32[]{:S(2)}) copy-start(f32[1,16,1]{1,2,0:T(1,128)} %get-tuple-element.2481) | copy-start | bytes 196 | tf_op jit(solution)/shard_map/transpose(jvp())/while
  313.6 9.9 %copy-start.10 = (f32[1,16,1]{1,2,0:T(1,128)S(1)}, f32[1,16,1]{1,2,0:T(1,128)}, u32[]{:S(2)}) copy-start(f32[1,16,1]{1,2,0:T(1,128)} %get-tuple-element.2481) | copy-start | bytes 196 | tf_op jit(solution)/shard_map/transpose(jvp())/while
  332.6 85.4 %reduce-scatter.5.cloned.1.call-start = ((), (), s32[]{:S(2)}) async-start(), calls=%async_computation.3 | async-start | bytes 589824 | tf_op jit(solution)/shard_map/reduce_scatter | solution.py:110
  339.3 7.3 %copy-start.3 = (bf16[4,256,16,64]{1,3,2,0:T(8,128)(2,1)S(1)}, bf16[4,256,16,64]{1,3,2,0:T(8,128)(2,1)}, u32[]{:S(2)}) copy-start(bf16[4,256,16,64]{1,3,2,0:T(8,128)(2,1)} %get-tuple-element.1014) | copy-start | bytes 6291460
Sparse Core Ops, SparseCore 0:
  19.0 80.3 all-gather.5
  102.0 76.7 all-gather.7
  332.7 46.2 reduce-scatter.2
  382.1 35.8 reduce-scatter.4
where the time goes:
time: 429 us; the launch traced here: 425 us
  local copies, waits for them, and re-layouts  147 us (34%)
  matrix products  74.1 us (17%)
  other arithmetic  68 us (16%)
  waiting for transfers between devices  61.6 us (14%)
  blocking collectives  56.2 us (13%)
  between operations  14.7 us (3%)
    unnamed x1, blocking collectives  56.2 us
    dynamic_slice x62, local copies, waits for them, and re-layouts, one(): lax.dynamic_index_in_dim(a, source, 0, False)  43.9 us
    unnamed x34, local copies, waits for them, and re-layouts  41.5 us
    reduce_scatter x1, waiting for transfers between devices, body(): lax.psum_scatter(grads[3], 'exp', scatter_dimension=0, tiled=True)  39 us
    dot_general x12, matrix products, advance(): jnp.einsum('hts,shp->thp', lowp(weights_ts), lowp(piece_x), preferred_ele...  36.3 us
    dynamic_update_slice x24, other arithmetic, mixer_blocks(): lax.scan(advance, entering, (split_x, split_rates, split_b, split_c))  28.1 us
    reduce_scatter x1, waiting for transfers between devices, body(): lax.psum_scatter(grads[2], 'exp', scatter_dimension=0, tiled=True)  21.1 us
    dynamic_update_slice x28, local copies, waits for them, and re-layouts, mixer_blocks(): lax.scan(advance, entering, (split_x, split_rates, split_b, split_c))  19.7 us
  transfers between devices with their start and end apart: 4, of which 3 were waited for; matrix products, arithmetic and copies ran while one was open for 30% of the time, Pallas kernels for 0%

commit v1 on v0

v1 whole, which is shorter than its diff:
```python
import functools

import jax
import jax.numpy as jnp
from jax import lax
from jax.experimental import pallas as pl
from jax.experimental.pallas import tpu as pltpu
from jax.sharding import PartitionSpec as P

F32 = jnp.float32
BF16 = jnp.bfloat16
MESH = pl.DeviceIdType.MESH
HEAD = 64
LANES = 128


def dot(a, b, ca, cb):
    return lax.dot_general(a, b, (((ca,), (cb,)), ((), ())), preferred_element_type=F32)


def nn(a, b):
    return dot(a, b, 1, 0)


def nt(a, b):
    return dot(a, b, 1, 1)


def tn(a, b):
    return dot(a, b, 0, 0)


def iota(shape, axis):
    return lax.broadcasted_iota(jnp.int32, shape, axis)


def pieces(value, count, axis):
    out = []
    for _ in range(count):
        part = value.astype(BF16)
        value = value - part.astype(F32)
        out.append(part)
    return jnp.concatenate(out, axis=axis)


def kernel(chips, ring, x_ref, ld_ref, b_ref, c_ref, skip_ref, dy_ref,
           y_ref, dx_ref, gld_ref, gb_ref, gc_ref,
           xs, ds, a_exp, inv_exp, gmat, hmat, sp, tp, mm, mt, dcs, dbs, bnd,
           spread, parts_a, parts_i, rows, lam, tri_s, skipe,
           state, grad, th, tb, lamh, lamp, pf, pb, cmf, cmb, rf, rb, esf, esb,
           ref_, reb, p2f, p2b, pef, peb, rsbuf,
           pair_s, pair_r, a2a_s, a2a_r, rs_s, rs_r):
    seq = lax.axis_index("seq")
    z = lax.axis_index("exp")
    core = lax.rem(seq, 2)
    chip = seq // 2
    other = 1 - core
    partner = (chip * 2 + other, z)
    heads = ld_ref.shape[0]
    length, width = x_ref.shape
    nc = ring
    q = length // nc
    state_n = b_ref.shape[1]
    pr = state_n // chips
    half = width // 2
    lb = half // LANES
    kh = nc * heads
    far = ring // 2

    def chip_dev(p):
        return (p * 2 + core, z)

    def at_chip(d):
        return lax.rem(chip + d, chips)

    barrier = pltpu.get_barrier_semaphore()
    pl.semaphore_signal(barrier, inc=1, device_id=partner, device_id_type=MESH)
    for d in range(1, chips):
        pl.semaphore_signal(barrier, inc=1, device_id=chip_dev(at_chip(d)), device_id_type=MESH)
    z_dn = lax.rem(z + ring - 1, ring)
    z_up = lax.rem(z + 1, ring)
    pl.semaphore_signal(barrier, inc=1, device_id=(seq, z_dn), device_id_type=MESH)
    pl.semaphore_signal(barrier, inc=1, device_id=(seq, z_up), device_id_type=MESH)

    def remote(src, dst, s_sem, r_sem, dev):
        return pltpu.make_async_remote_copy(
            src_ref=src, dst_ref=dst, send_sem=s_sem, recv_sem=r_sem,
            device_id=dev, device_id_type=MESH)

    stacked = jnp.concatenate([ld_ref[:, c * q:(c + 1) * q] for c in range(nc)], axis=0)
    tri = (iota((q, q), 0) >= iota((q, q), 1)).astype(BF16)
    cum = nt(jnp.concatenate([tri] * 3, axis=1), pieces(stacked, 3, 1))
    tri_s[...] = jnp.concatenate([tri] * 3, axis=0)
    rho = cum[q // 2 - 1:q // 2, :]
    tot = cum[q - 1:q, :]
    shifted = cum - rho
    parts_a[...] = pieces(jnp.exp(shifted), 2, 1)
    parts_i[...] = pieces(jnp.exp(-shifted), 2, 1)
    one = (lax.rem(iota((kh, width), 0), heads) == iota((kh, width), 1) // HEAD).astype(BF16)
    spread[...] = jnp.concatenate([one, one], axis=0)
    own_row = iota((nc, kh), 1) // heads == iota((nc, kh), 0)
    pair_rows = jnp.concatenate(
        [jnp.where(own_row, jnp.exp(rho), 0.0), jnp.where(own_row, jnp.exp(tot - rho), 0.0)], axis=0)
    rows[...] = nn(pieces(pair_rows, 3, 1), jnp.concatenate([one, one, one], axis=0))
    both = rows[0:nc, :] * rows[nc:2 * nc, :]
    total = both[0:1, :]
    for c in range(1, nc):
        total = total * both[c:c + 1, :]
    lam[...] = total
    for h in range(2):
        for r in range(lb):
            lamh[h, r:r + 1, :] = total[:, h * half + r * LANES:h * half + (r + 1) * LANES]
    head_one = (iota((heads, width), 1) // HEAD == iota((heads, width), 0)).astype(BF16)
    skipe[...] = nn(pieces(skip_ref[...], 3, 1), jnp.concatenate([head_one] * 3, axis=0))

    pl.semaphore_wait(barrier, chips + 2)
    send_lam = remote(lamh.at[other], lamp, pair_s.at[0], pair_r.at[0], partner)
    send_lam.start()

    def rows_of(c):
        return pl.ds(pl.multiple_of(c * q, q), q)

    lane_chunk = lax.rem(iota((q, 2 * kh), 1), kh) // heads

    state[...] = jnp.zeros_like(state)
    grad[...] = jnp.zeros_like(grad)

    def fwd_local(c, _):
        inv = nn(jnp.where(lane_chunk == c, parts_i[...], jnp.zeros((), BF16)), spread[...])
        inv_exp[c] = inv
        scaled = (x_ref[rows_of(c), :].astype(F32) * inv).astype(BF16)
        xs[c] = scaled
        got = tn(b_ref[rows_of(c), :], scaled)
        gmat[c] = got
        f = rows[pl.ds(c, 1), :]
        g = rows[pl.ds(nc + c, 1), :]
        state[...] = g * (f * state[...] + got)
        return 0

    def bwd_local(i, _):
        c = nc - 1 - i
        a = nn(jnp.where(lane_chunk == c, parts_a[...], jnp.zeros((), BF16)), spread[...])
        a_exp[c] = a
        scaled = (dy_ref[rows_of(c), :].astype(F32) * a).astype(BF16)
        ds[c] = scaled
        got = tn(c_ref[rows_of(c), :], scaled)
        hmat[c] = got
        f = rows[pl.ds(c, 1), :]
        g = rows[pl.ds(nc + c, 1), :]
        grad[...] = f * (g * grad[...] + got)
        return 0

    def to_halves(src, dst):
        for h in range(2):
            for r in range(lb):
                lo = h * half + r * LANES
                dst[h, r] = src[:, lo:lo + LANES].reshape(chips, pr, LANES)

    def lane_row(ref, r):
        return ref[r:r + 1, :].reshape(1, 1, LANES)

    lax.fori_loop(0, nc, fwd_local, 0)
    to_halves(state, th)
    send_pf = remote(th.at[other], pf, pair_s.at[1], pair_r.at[1], partner)
    send_pf.start()
    lax.fori_loop(0, nc, bwd_local, 0)
    to_halves(grad, tb)
    send_pb = remote(tb.at[other], pb, pair_s.at[2], pair_r.at[2], partner)
    send_pb.start()

    first = core == 0

    send_lam.wait_recv()
    send_pf.wait_recv()
    for r in range(lb):
        lo_, lp_ = lamh[core, r:r + 1, :].reshape(1, 1, LANES), lane_row(lamp, r)
        mine, theirs = th[core, r], pf[r]
        chip_t = jnp.where(first, lp_, 1.0) * mine + jnp.where(first, 1.0, lo_) * theirs
        cmf[:, r * pr:(r + 1) * pr, :] = chip_t
        cmf[:, lb * pr + r:lb * pr + r + 1, :] = jnp.broadcast_to(lo_ * lp_, (chips, 1, LANES))

    def exchange(src_of, dst, sems, base):
        out = []
        for d in range(1, chips):
            p = at_chip(d)
            out.append(remote(src_of.at[p], dst.at[chip], a2a_s.at[base, d], a2a_r.at[base, d], chip_dev(p)))
        for copy in out:
            copy.start()
        dst[chip] = src_of[chip]
        return out

    go_f = exchange(cmf, rf, None, 0)

    send_pb.wait_recv()
    for r in range(lb):
        lo_, lp_ = lamh[core, r:r + 1, :].reshape(1, 1, LANES), lane_row(lamp, r)
        mine, theirs = tb[core, r], pb[r]
        cmb[:, r * pr:(r + 1) * pr, :] = (
            jnp.where(first, 1.0, lp_) * mine + jnp.where(first, lo_, 1.0) * theirs)
    go_b = exchange(cmb, rb, None, 1)

    lower = iota((q, q), 0) >= iota((q, q), 1)
    upper = iota((q, q), 0) <= iota((q, q), 1)

    def inner(c, _):
        bb, cc = b_ref[rows_of(c), :], c_ref[rows_of(c), :]
        mm[c] = jnp.where(lower, nt(cc, bb), 0.0).astype(BF16)
        mt[c] = jnp.where(upper, nt(bb, cc), 0.0).astype(BF16)
        dm = jnp.where(lower, nt(ds[c], xs[c]), 0.0).astype(BF16)
        dcs[c] = nn(dm, bb)
        dbs[c] = tn(dm, cc)
        return 0

    lax.fori_loop(0, nc // 2, inner, 0)

    for copy in go_f:
        copy.wait_recv()
    run = [jnp.zeros((pr, LANES), F32) for _ in range(lb)]
    for p in range(chips):
        for r in range(lb):
            esf[p, r * pr:(r + 1) * pr, :] = run[r]
            run[r] = rf[p, lb * pr + r:lb * pr + r + 1, :] * run[r] + rf[p, r * pr:(r + 1) * pr, :]
    ret_f = exchange(esf, ref_, None, 2)

    for copy in go_b:
        copy.wait_recv()
    run = [jnp.zeros((pr, LANES), F32) for _ in range(lb)]
    for p in reversed(range(chips)):
        for r in range(lb):
            esb[p, r * pr:(r + 1) * pr, :] = run[r]
            run[r] = rf[p, lb * pr + r:lb * pr + r + 1, :] * run[r] + rb[p, r * pr:(r + 1) * pr, :]
    ret_b = exchange(esb, reb, None, 3)

    lax.fori_loop(nc // 2, nc, inner, 0)

    def place(dst, r, lane_half, value):
        lo = pl.multiple_of(lane_half * half + r * LANES, LANES)
        dst[:, pl.ds(lo, LANES)] = value.reshape(state_n, LANES)

    for copy in ret_f:
        copy.wait_recv()
    for r in range(lb):
        lo_, lp_ = lamh[core, r:r + 1, :].reshape(1, 1, LANES), lane_row(lamp, r)
        enter = ref_[:, r * pr:(r + 1) * pr, :]
        later = jnp.where(first, lo_, lp_) * enter + jnp.where(first, th[core, r], pf[r])
        p2f[r] = jnp.where(first, later, enter)
        place(state, r, core, jnp.where(first, enter, later))
    send_2f = remote(p2f, pef, pair_s.at[3], pair_r.at[3], partner)
    send_2f.start()

    for copy in ret_b:
        copy.wait_recv()
    for r in range(lb):
        lo_, lp_ = lamh[core, r:r + 1, :].reshape(1, 1, LANES), lane_row(lamp, r)
        enter = reb[:, r * pr:(r + 1) * pr, :]
        earlier = jnp.where(first, lp_, lo_) * enter + jnp.where(first, pb[r], tb[core, r])
        p2b[r] = jnp.where(first, enter, earlier)
        place(grad, r, core, jnp.where(first, earlier, enter))
    send_2b = remote(p2b, peb, pair_s.at[4], pair_r.at[4], partner)
    send_2b.start()

    send_2f.wait_recv()
    for r in range(lb):
        place(state, r, other, pef[r])

    def fwd_state(c, _):
        f = rows[pl.ds(c, 1), :]
        g = rows[pl.ds(nc + c, 1), :]
        entering = f * state[...]
        sp[c] = entering.astype(BF16)
        leaving = entering + gmat[c]
        gmat[c] = leaving
        state[...] = g * leaving
        return 0

    lax.fori_loop(0, nc, fwd_state, 0)

    hq = q // 2

    def rs_copy(t, way, step, src):
        to = (seq, z_dn if way == 0 else z_up)
        dst = rsbuf.at[t, way, step]
        if step == 0:
            dst = dst.at[pl.ds(way * hq, hq)]
        return remote(src, dst, rs_s.at[t, way, step], rs_r.at[t, way, step], to)

    def chunk_at(way, step):
        gap = far - step
        return lax.rem(z + (ring - gap if way == 0 else gap), ring)

    started = {}

    def rs_start(t, own):
        for way in range(2):
            src = own.at[chunk_at(way, 0), pl.ds(way * hq, hq)]
            started[t, way, 0] = rs_copy(t, way, 0, src)
            started[t, way, 0].start()

    def rs_next(t, own, step):
        for way in range(2):
            started[t, way, step - 1].wait_recv()
            k = chunk_at(way, step)
            if step == 1:
                lo = way * hq
                rsbuf[t, way, 0, lo:lo + hq, :] += own[k, lo:lo + hq, :]
                lo = hq - lo
                rsbuf[t, way, 0, lo:lo + hq, :] = own[k, lo:lo + hq, :]
            else:
                rsbuf[t, way, step - 1] += own[k]
            started[t, way, step] = rs_copy(t, way, step, rsbuf.at[t, way, step - 1])
            started[t, way, step].start()

    def rs_end(t, own, out):
        for way in range(2):
            started[t, way, far - 1].wait_recv()
        last = rsbuf[t, 0, far - 1] + rsbuf[t, 1, far - 1]
        if far == 1:
            raise ValueError("ring")
        out[...] = own[z] + last

    def dc_chunk(i, _):
        c = lax.rem(z + far + i, ring)
        dcs[c] += nt(ds[c], sp[c])
        return 0

    def db_chunk(i, _):
        c = lax.rem(z + far + i, ring)
        dbs[c] += nt(xs[c], tp[c])
        return 0

    dc_chunk(0, 0)
    rs_start(0, dcs)
    lax.fori_loop(1, nc, dc_chunk, 0)

    send_2b.wait_recv()
    for r in range(lb):
        place(grad, r, other, peb[r])

    def bwd_state(i, _):
        c = nc - 1 - i
        f = rows[pl.ds(c, 1), :]
        g = rows[pl.ds(nc + c, 1), :]
        later = g * grad[...]
        low = later.astype(BF16)
        tp[c] = low
        bnd[pl.ds(c, 1), :] = jnp.sum(low.astype(F32) * gmat[c], axis=0, keepdims=True)
        grad[...] = f * (later + hmat[c])
        return 0

    lax.fori_loop(0, nc, bwd_state, 0)
    rs_next(0, dcs, 1)
    db_chunk(0, 0)
    rs_start(1, dbs)
    lax.fori_loop(1, nc, db_chunk, 0)

    last_row = iota((q, width), 0) == q - 1

    def outputs(c, _):
        x_c, d_c = xs[c], ds[c]
        acc_y = nn(jnp.concatenate([mm[c], c_ref[rows_of(c), :]], axis=1),
                   jnp.concatenate([x_c, sp[c]], axis=0))
        acc_x = nn(jnp.concatenate([mt[c], b_ref[rows_of(c), :]], axis=1),
                   jnp.concatenate([d_c, tp[c]], axis=0))
        gain = skipe[...]
        y_ref[rows_of(c), :] = (a_exp[c] * acc_y + gain * x_ref[rows_of(c), :].astype(F32)).astype(BF16)
        dx_ref[rows_of(c), :] = (inv_exp[c] * acc_x + gain * dy_ref[rows_of(c), :].astype(F32)).astype(BF16)
        diff = d_c.astype(F32) * acc_y - x_c.astype(F32) * acc_x
        diff = diff + jnp.where(last_row, bnd[pl.ds(c, 1), :], 0.0)
        hi = diff.astype(BF16)
        lo = (diff - hi.astype(F32)).astype(BF16)
        per_head = nt(head_one, hi) + nt(head_one, lo)
        gld_ref[:, rows_of(c)] = nn(pieces(per_head, 3, 1), tri_s[...])
        return 0

    done = 0
    for step in range(1, far):
        upto = nc * step // far
        lax.fori_loop(done, upto, outputs, 0)
        done = upto
        if step + 1 < far:
            rs_next(0, dcs, step + 1)
        rs_next(1, dbs, step)
    lax.fori_loop(done, nc, outputs, 0)
    rs_end(0, dcs, gc_ref)
    rs_end(1, dbs, gb_ref)

    for copy in [send_lam, send_pf, send_pb, send_2f, send_2b, *go_f, *go_b, *ret_f, *ret_b,
                 *started.values()]:
        copy.wait_send()


def body(chips, ring, mixer_input, log_decay, b_rows, c_rows, skip_gain, grad_out):
    length, width = mixer_input.shape
    heads = log_decay.shape[0]
    state_n = b_rows.shape[1]
    nc = ring
    q = length // nc
    kh = nc * heads
    pr = state_n // chips
    lb = width // 2 // LANES
    far = ring // 2
    vm = pltpu.VMEM
    piece = (lb, chips, pr, LANES)
    msg = (chips, lb * pr, LANES)
    msg_l = (chips, lb * pr + 8, LANES)
    scratch = [
        vm((nc, q, width), BF16), vm((nc, q, width), BF16),
        vm((nc, q, width), F32), vm((nc, q, width), F32),
        vm((nc, state_n, width), F32), vm((nc, state_n, width), F32),
        vm((nc, state_n, width), BF16), vm((nc, state_n, width), BF16),
        vm((nc, q, q), BF16), vm((nc, q, q), BF16),
        vm((nc, q, state_n), F32), vm((nc, q, state_n), F32),
        vm((nc, width), F32),
        vm((2 * kh, width), BF16), vm((q, 2 * kh), BF16), vm((q, 2 * kh), BF16),
        vm((2 * nc, width), F32), vm((1, width), F32), vm((3 * q, q), BF16), vm((1, width), F32),
        vm((state_n, width), F32), vm((state_n, width), F32),
        vm((2, *piece), F32), vm((2, *piece), F32), vm((2, 8, LANES), F32), vm((8, LANES), F32),
        vm(piece, F32), vm(piece, F32),
        vm(msg_l, F32), vm(msg, F32), vm(msg_l, F32), vm(msg, F32), vm(msg, F32), vm(msg, F32),
        vm(msg, F32), vm(msg, F32), vm(piece, F32), vm(piece, F32), vm(piece, F32), vm(piece, F32),
        vm((2, 2, far, q, state_n), F32),
        pltpu.SemaphoreType.DMA((5,)), pltpu.SemaphoreType.DMA((5,)),
        pltpu.SemaphoreType.DMA((4, chips)), pltpu.SemaphoreType.DMA((4, chips)),
        pltpu.SemaphoreType.DMA((2, 2, far)), pltpu.SemaphoreType.DMA((2, 2, far)),
    ]
    whole = pl.BlockSpec(memory_space=pltpu.VMEM)
    return pl.pallas_call(
        functools.partial(kernel, chips, ring),
        out_shape=(
            jax.ShapeDtypeStruct((length, width), BF16),
            jax.ShapeDtypeStruct((length, width), BF16),
            jax.ShapeDtypeStruct((heads, length), F32),
            jax.ShapeDtypeStruct((q, state_n), F32),
            jax.ShapeDtypeStruct((q, state_n), F32),
        ),
        in_specs=[whole] * 6,
        out_specs=(whole,) * 5,
        scratch_shapes=scratch,
        compiler_params=pltpu.CompilerParams(
            collective_id=0, has_side_effects=True, vmem_limit_bytes=60 * 1024 * 1024),
    )(mixer_input, log_decay, b_rows, c_rows, skip_gain.reshape(1, heads), grad_out)


def solution(mesh):
    chips = mesh.shape["seq"] // 2
    ring = mesh.shape["exp"]
    return jax.shard_map(
        functools.partial(body, chips, ring),
        mesh=mesh,
        in_specs=(
            P("seq", "exp"),
            P("exp", "seq"),
            P("seq", None),
            P("seq", None),
            P("exp"),
            P("seq", "exp"),
        ),
        out_specs=(
            P("seq", "exp"),
            P("seq", "exp"),
            P("exp", "seq"),
            P(("seq", "exp"), None),
            P(("seq", "exp"), None),
        ),
        check_vma=False,
    )
```

time: 429 us -> 66.4 us (0.15)
  local copies, waits for them, and re-layouts: 147 us -> 6.45 us
  matrix products: 74.1 us -> 0 us
  other arithmetic: 68 us -> 0 us
  waiting for transfers between devices: 61.6 us -> 0 us
  Pallas kernels: 0 us -> 58.3 us
  blocking collectives: 56.2 us -> 0 us
  between operations: 14.7 us -> 0.66 us
    dot_general x46 -> x0, matrix products: 73 us -> none  [the longest x12 36.3 us: advance(): jnp.einsum('hts,shp->thp', lowp(weights_ts), lowp(piece_x), preferred_ele...]
    dynamic_slice x82 -> x0, local copies, waits for them, and re-layouts: 60.9 us -> none  [the longest x62 43.9 us: one(): lax.dynamic_index_in_dim(a, source, 0, False)]
    reduce_scatter x2 -> x0, waiting for transfers between devices: 60.1 us -> none  [the longest x1 39 us: body(): lax.psum_scatter(grads[3], 'exp', scatter_dimension=0, tiled=True)]
    pallas_call x0 -> x1, Pallas kernels: none -> 58.3 us  [body(): pl.pallas_call(functools.partial(kernel, chips, ring), out_shape=(jax.Sha...]
    unnamed x1 -> x0, blocking collectives: 56.2 us -> none
    unnamed x34 -> x13, local copies, waits for them, and re-layouts: 41.5 us -> 6.45 us
    dynamic_update_slice x24 -> x0, other arithmetic: 28.1 us -> none  [mixer_blocks(): lax.scan(advance, entering, (split_x, split_rates, split_b, split_c))]
    dynamic_update_slice x28 -> x0, local copies, waits for them, and re-layouts: 19.7 us -> none  [mixer_blocks(): lax.scan(advance, entering, (split_x, split_rates, split_b, split_c))]
  transfers between devices with their start and end apart: 4 -> 0, of which waited for: 3 -> 0; matrix products, arithmetic and copies ran while one was open for 30% -> 0% of each run, Pallas kernels for 0% -> 0%
where the time goes in v1:
time: 66.4 us; the launch traced here: 65.4 us
  Pallas kernels  58.3 us (88%)
  local copies, waits for them, and re-layouts  6.45 us (10%)
    pallas_call x1, Pallas kernels, body(): pl.pallas_call(functools.partial(kernel, chips, ring), out_shape=(jax.Sha...  58.3 us
    unnamed x13, local copies, waits for them, and re-layouts  6.45 us

profile of v1, /device:TPU:8, one launch (start us, length us, event | category | flops | bytes accessed | tf_op | source)
XLA Modules:
  0.0 65.4 jit_solution(718482800467486176)
XLA Ops:
  0.6 58.3 %shard_map.101 = (bf16[1024,1024]{1,0:T(8,128)(2,1)}, bf16[1024,1024]{1,0:T(8,128)(2,1)}, f32[16,1024]{1,0:T(8,128)}, f32[128,128]{1,0:T(8,128)}, f32[128,128]{1,0:T(8,128)}) custom-call(bf16[1024,1024]{1,0:T(8,128)(2,1)} %x_ref.1, f32[16,1024]{1,0:T(8,128)} %ld_ref.1, bf16[1024,128]{1,0:T(8,128)(2,1)} %b_ref.1, bf16[1024,128]{1,0:T(8,128)(2,1)} %c_ref.1, ...), custom_call_target="tpu_custom_call" | custom-call | tf_op jit(solution)/shard_map/pallas_call | solution.py:427
  58.9 0.0 copy-start
  58.9 3.2 %copy.16 = bf16[1024,1024]{1,0:T(8,128)(2,1)} copy(bf16[1024,1024]{1,0:T(8,128)(2,1)} %get-tuple-element.10) | data formatting | bytes 4194304
  62.2 0.0 copy-done
  62.2 0.0 copy-start.3
  62.2 0.0 copy-start.2
  62.2 0.0 copy-start.1
  62.2 1.3 %copy.17 = bf16[1024,1024]{1,0:T(8,128)(2,1)} copy(bf16[1024,1024]{1,0:T(8,128)(2,1)S(1)} %copy-done) | data formatting | bytes 4194304
  63.5 0.0 copy-done.3
  63.5 0.6 copy.18
  64.1 0.0 copy-done.2
  64.1 0.6 copy.19
  64.8 0.0 copy-done.1
  64.8 0.6 copy.20
Async XLA Ops:
  58.9 3.2 %copy-start = (bf16[1024,1024]{1,0:T(8,128)(2,1)S(1)}, bf16[1024,1024]{1,0:T(8,128)(2,1)}, u32[]{:S(2)}) copy-start(bf16[1024,1024]{1,0:T(8,128)(2,1)} %get-tuple-element.11) | copy-start | bytes 6291460
  62.2 1.3 %copy-start.3 = (f32[16,1024]{1,0:T(8,128)S(1)}, f32[16,1024]{1,0:T(8,128)}, u32[]{:S(2)}) copy-start(f32[16,1024]{1,0:T(8,128)} %get-tuple-element.12) | copy-start | bytes 196612
  62.2 2.0 %copy-start.2 = (f32[128,128]{1,0:T(8,128)S(1)}, f32[128,128]{1,0:T(8,128)}, u32[]{:S(2)}) copy-start(f32[128,128]{1,0:T(8,128)} %get-tuple-element.13) | copy-start | bytes 196612
  62.2 2.6 %copy-start.1 = (f32[128,128]{1,0:T(8,128)S(1)}, f32[128,128]{1,0:T(8,128)}, u32[]{:S(2)}) copy-start(f32[128,128]{1,0:T(8,128)} %get-tuple-element.14) | copy-start | bytes 196612

commit v2 on v1

--- a/solution.py
+++ b/solution.py
@@ -43,13 +43,14 @@
     return jnp.concatenate(out, axis=axis)
 
 
-def kernel(chips, ring, x_ref, ld_ref, b_ref, c_ref, skip_ref, dy_ref,
+def kernel(chips, ring, x_ref, ld_ref, b_any, c_any, skip_ref, dy_ref,
            y_ref, dx_ref, gld_ref, gb_ref, gc_ref,
+           xv, dyv, b_ref, c_ref, yv, dxv,
            xs, ds, a_exp, inv_exp, gmat, hmat, sp, tp, mm, mt, dcs, dbs, bnd,
            spread, parts_a, parts_i, rows, lam, tri_s, skipe,
            state, grad, th, tb, lamh, lamp, pf, pb, cmf, cmb, rf, rb, esf, esb,
            ref_, reb, p2f, p2b, pef, peb, rsbuf,
-           pair_s, pair_r, a2a_s, a2a_r, rs_s, rs_r):
+           in_s, out_s, lam_s, lam_r, pair_s, pair_r, a2a_s, a2a_r, rs_s, rs_r):
     seq = lax.axis_index("seq")
     z = lax.axis_index("exp")
     core = lax.rem(seq, 2)
@@ -60,6 +61,9 @@
     length, width = x_ref.shape
     nc = ring
     q = length // nc
+    nx = min(4, chips)
+    ny = chips // nx
+    cx, cy = lax.rem(chip, nx), chip // nx
     state_n = b_ref.shape[1]
     pr = state_n // chips
     half = width // 2
@@ -70,13 +74,23 @@
     def chip_dev(p):
         return (p * 2 + core, z)
 
-    def at_chip(d):
-        return lax.rem(chip + d, chips)
+    offsets = sorted(
+        [(dy, dx) for dy in range(ny) for dx in range(nx) if (dy, dx) != (0, 0)],
+        key=lambda o: (min(o[0], ny - o[0]) + min(o[1], nx - o[1]), o[0]))
+    count = len(offsets)
+
+    def chip_to(d):
+        dy, dx = offsets[d]
+        return lax.rem(cy + dy, ny) * nx + lax.rem(cx + dx, nx)
+
+    def chip_from(d):
+        dy, dx = offsets[d]
+        return lax.rem(cy + ny - dy, ny) * nx + lax.rem(cx + nx - dx, nx)
 
     barrier = pltpu.get_barrier_semaphore()
     pl.semaphore_signal(barrier, inc=1, device_id=partner, device_id_type=MESH)
-    for d in range(1, chips):
-        pl.semaphore_signal(barrier, inc=1, device_id=chip_dev(at_chip(d)), device_id_type=MESH)
+    for d in range(count):
+        pl.semaphore_signal(barrier, inc=1, device_id=chip_dev(chip_to(d)), device_id_type=MESH)
     z_dn = lax.rem(z + ring - 1, ring)
     z_up = lax.rem(z + 1, ring)
     pl.semaphore_signal(barrier, inc=1, device_id=(seq, z_dn), device_id_type=MESH)
@@ -86,6 +100,22 @@
         return pltpu.make_async_remote_copy(
             src_ref=src, dst_ref=dst, send_sem=s_sem, recv_sem=r_sem,
             device_id=dev, device_id_type=MESH)
+
+    def rows_of(c):
+        return pl.ds(pl.multiple_of(c * q, q), q)
+
+    def loads(k, src, dst, c):
+        return pltpu.make_async_copy(src.at[rows_of(c)], dst.at[rows_of(c)], in_s.at[k, c])
+
+    def whole_load(k):
+        return pltpu.make_async_copy((b_any, c_any)[k], (b_ref, c_ref)[k], in_s.at[k, nc])
+
+    whole_load(0).start()
+    for c in range(nc):
+        loads(0, x_ref, xv, c).start()
+    whole_load(1).start()
+    for c in reversed(range(nc)):
+        loads(1, dy_ref, dyv, c).start()
 
     stacked = jnp.concatenate([ld_ref[:, c * q:(c + 1) * q] for c in range(nc)], axis=0)
     tri = (iota((q, q), 0) >= iota((q, q), 1)).astype(BF16)
@@ -113,13 +143,6 @@
     head_one = (iota((heads, width), 1) // HEAD == iota((heads, width), 0)).astype(BF16)
     skipe[...] = nn(pieces(skip_ref[...], 3, 1), jnp.concatenate([head_one] * 3, axis=0))
 
-    pl.semaphore_wait(barrier, chips + 2)
-    send_lam = remote(lamh.at[other], lamp, pair_s.at[0], pair_r.at[0], partner)
-    send_lam.start()
-
-    def rows_of(c):
-        return pl.ds(pl.multiple_of(c * q, q), q)
-
     lane_chunk = lax.rem(iota((q, 2 * kh), 1), kh) // heads
 
     state[...] = jnp.zeros_like(state)
@@ -128,7 +151,8 @@
     def fwd_local(c, _):
         inv = nn(jnp.where(lane_chunk == c, parts_i[...], jnp.zeros((), BF16)), spread[...])
         inv_exp[c] = inv
-        scaled = (x_ref[rows_of(c), :].astype(F32) * inv).astype(BF16)
+        loads(0, x_ref, xv, c).wait()
+        scaled = (xv[rows_of(c), :].astype(F32) * inv).astype(BF16)
         xs[c] = scaled
         got = tn(b_ref[rows_of(c), :], scaled)
         gmat[c] = got
@@ -141,7 +165,8 @@
         c = nc - 1 - i
         a = nn(jnp.where(lane_chunk == c, parts_a[...], jnp.zeros((), BF16)), spread[...])
         a_exp[c] = a
-        scaled = (dy_ref[rows_of(c), :].astype(F32) * a).astype(BF16)
+        loads(1, dy_ref, dyv, c).wait()
+        scaled = (dyv[rows_of(c), :].astype(F32) * a).astype(BF16)
         ds[c] = scaled
         got = tn(c_ref[rows_of(c), :], scaled)
         hmat[c] = got
@@ -154,50 +179,102 @@
         for h in range(2):
             for r in range(lb):
                 lo = h * half + r * LANES
-                dst[h, r] = src[:, lo:lo + LANES].reshape(chips, pr, LANES)
-
-    def lane_row(ref, r):
-        return ref[r:r + 1, :].reshape(1, 1, LANES)
-
-    lax.fori_loop(0, nc, fwd_local, 0)
-    to_halves(state, th)
-    send_pf = remote(th.at[other], pf, pair_s.at[1], pair_r.at[1], partner)
-    send_pf.start()
-    lax.fori_loop(0, nc, bwd_local, 0)
-    to_halves(grad, tb)
-    send_pb = remote(tb.at[other], pb, pair_s.at[2], pair_r.at[2], partner)
-    send_pb.start()
+                dst[h, :, r * pr:(r + 1) * pr, :] = src[:, lo:lo + LANES].reshape(chips, pr, LANES)
 
     first = core == 0
 
-    send_lam.wait_recv()
-    send_pf.wait_recv()
-    for r in range(lb):
-        lo_, lp_ = lamh[core, r:r + 1, :].reshape(1, 1, LANES), lane_row(lamp, r)
-        mine, theirs = th[core, r], pf[r]
-        chip_t = jnp.where(first, lp_, 1.0) * mine + jnp.where(first, 1.0, lo_) * theirs
-        cmf[:, r * pr:(r + 1) * pr, :] = chip_t
-        cmf[:, lb * pr + r:lb * pr + r + 1, :] = jnp.broadcast_to(lo_ * lp_, (chips, 1, LANES))
-
-    def exchange(src_of, dst, sems, base):
+    def piece_of(d):
+        return chip_to(d) if d < count else chip
+
+    def pair_send(base, src, dst, which):
         out = []
-        for d in range(1, chips):
-            p = at_chip(d)
-            out.append(remote(src_of.at[p], dst.at[chip], a2a_s.at[base, d], a2a_r.at[base, d], chip_dev(p)))
-        for copy in out:
+        for d in range(count + 1):
+            p = which(d)
+            out.append(remote(src.at[p], dst.at[p], pair_s.at[base, d], pair_r.at[base, d], partner))
+            out[-1].start()
+        return out
+
+    def pass_on(base, d, src, dst, p):
+        copy = remote(src.at[p], dst.at[chip], a2a_s.at[base, d], a2a_r.at[base, d], chip_dev(p))
+        copy.start()
+        return copy
+
+    def lam_rows():
+        return ([lamh[core, r:r + 1, :] for r in range(lb)], [lamp[r:r + 1, :] for r in range(lb)])
+
+    def combine(base, came, kept, got, out, dst, forward):
+        lo_, lp_ = lam_rows()
+        go = []
+        for d in range(count + 1):
+            p = piece_of(d)
+            came[d].wait_recv()
+            for r in range(lb):
+                lanes = slice(r * pr, (r + 1) * pr)
+                mine, theirs = kept[core, p, lanes, :], got[p, lanes, :]
+                if forward:
+                    value = jnp.where(first, lp_[r], 1.0) * mine + jnp.where(first, 1.0, lo_[r]) * theirs
+                else:
+                    value = jnp.where(first, 1.0, lp_[r]) * mine + jnp.where(first, lo_[r], 1.0) * theirs
+                if d < count:
+                    out[p, lanes, :] = value
+                else:
+                    dst[chip, lanes, :] = value
+            if forward:
+                for r in range(lb):
+                    row = slice(lb * pr + r, lb * pr + r + 1)
+                    if d < count:
+                        out[p, row, :] = lo_[r] * lp_[r]
+                    else:
+                        dst[chip, row, :] = lo_[r] * lp_[r]
+            if d < count:
+                go.append(pass_on(base, d, out, dst, p))
+        return go
+
+    def scan_pieces(go, base, got, out, dst, order):
+        for copy in go:
+            copy.wait_recv()
+        run = [jnp.zeros((pr, LANES), F32) for _ in range(lb)]
+        for p in order:
+            for r in range(lb):
+                out[p, r * pr:(r + 1) * pr, :] = run[r]
+                run[r] = rf[p, lb * pr + r:lb * pr + r + 1, :] * run[r] + got[p, r * pr:(r + 1) * pr, :]
+        dst[chip] = out[chip]
+        return [pass_on(base, d, out, dst, chip_to(d)) for d in range(count)]
+
+    def place(dst, p, r, lane_half, value):
+        lo = pl.multiple_of(lane_half * half + r * LANES, LANES)
+        dst[pl.ds(pl.multiple_of(p * pr, pr), pr), pl.ds(lo, LANES)] = value
+
+    def hand_out(base, ret, enters, kept, got, share, shared, dst, forward):
+        lo_, lp_ = lam_rows()
+        out = []
+        for d in [count, *range(count)]:
+            p = chip_from(d) if d < count else chip
+            if d < count:
+                ret[d].wait_recv()
+            for r in range(lb):
+                lanes = slice(r * pr, (r + 1) * pr)
+                enter = enters[p, lanes, :]
+                if forward:
+                    past = jnp.where(first, lo_[r], lp_[r]) * enter + jnp.where(
+                        first, kept[core, p, lanes, :], got[p, lanes, :])
+                    own, theirs = jnp.where(first, enter, past), jnp.where(first, past, enter)
+                else:
+                    past = jnp.where(first, lp_[r], lo_[r]) * enter + jnp.where(
+                        first, got[p, lanes, :], kept[core, p, lanes, :])
+                    own, theirs = jnp.where(first, past, enter), jnp.where(first, enter, past)
+                share[p, lanes, :] = theirs
+                place(dst, p, r, core, own)
+            copy = remote(share.at[p], shared.at[p], pair_s.at[base, d], pair_r.at[base, d], partner)
             copy.start()
-        dst[chip] = src_of[chip]
+            out.append((p, copy))
         return out
 
-    go_f = exchange(cmf, rf, None, 0)
-
-    send_pb.wait_recv()
-    for r in range(lb):
-        lo_, lp_ = lamh[core, r:r + 1, :].reshape(1, 1, LANES), lane_row(lamp, r)
-        mine, theirs = tb[core, r], pb[r]
-        cmb[:, r * pr:(r + 1) * pr, :] = (
-            jnp.where(first, 1.0, lp_) * mine + jnp.where(first, lo_, 1.0) * theirs)
-    go_b = exchange(cmb, rb, None, 1)
+    def take_in(pairs, shared, dst):
+        for p, copy in pairs:
+            copy.wait_recv()
+            for r in range(lb):
+                place(dst, p, r, other, shared[p, r * pr:(r + 1) * pr, :])
 
     lower = iota((q, q), 0) >= iota((q, q), 1)
     upper = iota((q, q), 0) <= iota((q, q), 1)
@@ -211,57 +288,29 @@
         dbs[c] = tn(dm, cc)
         return 0
 
-    lax.fori_loop(0, nc // 2, inner, 0)
-
-    for copy in go_f:
-        copy.wait_recv()
-    run = [jnp.zeros((pr, LANES), F32) for _ in range(lb)]
-    for p in range(chips):
-        for r in range(lb):
-            esf[p, r * pr:(r + 1) * pr, :] = run[r]
-            run[r] = rf[p, lb * pr + r:lb * pr + r + 1, :] * run[r] + rf[p, r * pr:(r + 1) * pr, :]
-    ret_f = exchange(esf, ref_, None, 2)
-
-    for copy in go_b:
-        copy.wait_recv()
-    run = [jnp.zeros((pr, LANES), F32) for _ in range(lb)]
-    for p in reversed(range(chips)):
-        for r in range(lb):
-            esb[p, r * pr:(r + 1) * pr, :] = run[r]
-            run[r] = rf[p, lb * pr + r:lb * pr + r + 1, :] * run[r] + rb[p, r * pr:(r + 1) * pr, :]
-    ret_b = exchange(esb, reb, None, 3)
-
-    lax.fori_loop(nc // 2, nc, inner, 0)
-
-    def place(dst, r, lane_half, value):
-        lo = pl.multiple_of(lane_half * half + r * LANES, LANES)
-        dst[:, pl.ds(lo, LANES)] = value.reshape(state_n, LANES)
-
-    for copy in ret_f:
-        copy.wait_recv()
-    for r in range(lb):
-        lo_, lp_ = lamh[core, r:r + 1, :].reshape(1, 1, LANES), lane_row(lamp, r)
-        enter = ref_[:, r * pr:(r + 1) * pr, :]
-        later = jnp.where(first, lo_, lp_) * enter + jnp.where(first, th[core, r], pf[r])
-        p2f[r] = jnp.where(first, later, enter)
-        place(state, r, core, jnp.where(first, enter, later))
-    send_2f = remote(p2f, pef, pair_s.at[3], pair_r.at[3], partner)
-    send_2f.start()
-
-    for copy in ret_b:
-        copy.wait_recv()
-    for r in range(lb):
-        lo_, lp_ = lamh[core, r:r + 1, :].reshape(1, 1, LANES), lane_row(lamp, r)
-        enter = reb[:, r * pr:(r + 1) * pr, :]
-        earlier = jnp.where(first, lp_, lo_) * enter + jnp.where(first, pb[r], tb[core, r])
-        p2b[r] = jnp.where(first, enter, earlier)
-        place(grad, r, core, jnp.where(first, earlier, enter))
-    send_2b = remote(p2b, peb, pair_s.at[4], pair_r.at[4], partner)
-    send_2b.start()
-
-    send_2f.wait_recv()
-    for r in range(lb):
-        place(state, r, other, pef[r])
+    whole_load(0).wait()
+    lax.fori_loop(0, nc, fwd_local, 0)
+    to_halves(state, th)
+    pl.semaphore_wait(barrier, chips + 2)
+    send_lam = remote(lamh.at[other], lamp, lam_s, lam_r, partner)
+    send_lam.start()
+    pair_f = pair_send(0, th.at[other], pf, piece_of)
+    whole_load(1).wait()
+    lax.fori_loop(0, nc // 2, bwd_local, 0)
+    send_lam.wait_recv()
+    go_f = combine(0, pair_f, th, pf, cmf, rf, True)
+    lax.fori_loop(nc // 2, nc, bwd_local, 0)
+    to_halves(grad, tb)
+    pair_b = pair_send(1, tb.at[other], pb, piece_of)
+    lax.fori_loop(0, nc // 4, inner, 0)
+    go_b = combine(1, pair_b, tb, pb, cmb, rb, False)
+    lax.fori_loop(nc // 4, nc // 2, inner, 0)
+    ret_f = scan_pieces(go_f, 2, rf, esf, ref_, range(chips))
+    lax.fori_loop(nc // 2, 3 * nc // 4, inner, 0)
+    ret_b = scan_pieces(go_b, 3, rb, esb, reb, list(reversed(range(chips))))
+    lax.fori_loop(3 * nc // 4, nc, inner, 0)
+    send_2f = hand_out(2, ret_f, ref_, th, pf, p2f, pef, state, True)
+    take_in(send_2f, pef, state)
 
     def fwd_state(c, _):
         f = rows[pl.ds(c, 1), :]
@@ -332,9 +381,8 @@
     rs_start(0, dcs)
     lax.fori_loop(1, nc, dc_chunk, 0)
 
-    send_2b.wait_recv()
-    for r in range(lb):
-        place(grad, r, other, peb[r])
+    send_2b = hand_out(3, ret_b, reb, tb, pb, p2b, peb, grad, False)
+    take_in(send_2b, peb, grad)
 
     def bwd_state(i, _):
         c = nc - 1 - i
@@ -355,6 +403,10 @@
 
     last_row = iota((q, width), 0) == q - 1
 
+    def stores(k, c):
+        src, dst = ((yv, y_ref), (dxv, dx_ref))[k]
+        return pltpu.make_async_copy(src.at[rows_of(c)], dst.at[rows_of(c)], out_s.at[k, c])
+
     def outputs(c, _):
         x_c, d_c = xs[c], ds[c]
         acc_y = nn(jnp.concatenate([mm[c], c_ref[rows_of(c), :]], axis=1),
@@ -362,14 +414,16 @@
         acc_x = nn(jnp.concatenate([mt[c], b_ref[rows_of(c), :]], axis=1),
                    jnp.concatenate([d_c, tp[c]], axis=0))
         gain = skipe[...]
-        y_ref[rows_of(c), :] = (a_exp[c] * acc_y + gain * x_ref[rows_of(c), :].astype(F32)).astype(BF16)
-        dx_ref[rows_of(c), :] = (inv_exp[c] * acc_x + gain * dy_ref[rows_of(c), :].astype(F32)).astype(BF16)
+        yv[rows_of(c), :] = (a_exp[c] * acc_y + gain * xv[rows_of(c), :].astype(F32)).astype(BF16)
+        dxv[rows_of(c), :] = (inv_exp[c] * acc_x + gain * dyv[rows_of(c), :].astype(F32)).astype(BF16)
         diff = d_c.astype(F32) * acc_y - x_c.astype(F32) * acc_x
         diff = diff + jnp.where(last_row, bnd[pl.ds(c, 1), :], 0.0)
         hi = diff.astype(BF16)
         lo = (diff - hi.astype(F32)).astype(BF16)
         per_head = nt(head_one, hi) + nt(head_one, lo)
         gld_ref[:, rows_of(c)] = nn(pieces(per_head, 3, 1), tri_s[...])
+        stores(0, c).start()
+        stores(1, c).start()
         return 0
 
     done = 0
@@ -384,9 +438,40 @@
     rs_end(0, dcs, gc_ref)
     rs_end(1, dbs, gb_ref)
 
-    for copy in [send_lam, send_pf, send_pb, send_2f, send_2b, *go_f, *go_b, *ret_f, *ret_b,
-                 *started.values()]:
+    for c in range(nc):
+        stores(0, c).wait()
+        stores(1, c).wait()
+    for copy in [send_lam, *pair_f, *pair_b, *go_f, *go_b, *ret_f, *ret_b,
+                 *[c for _, c in send_2f], *[c for _, c in send_2b], *started.values()]:
         copy.wait_send()
+
+
+def finish_kernel(*refs):
+    count = (len(refs) - 1) // 2
+    sems = refs[-1]
+    copies = []
+    for k in range(count):
+        src, dst = refs[k], refs[count + k]
+        parts = 4 if src.shape[0] >= 1024 else 1
+        size = src.shape[0] // parts
+        for i in range(parts):
+            rows = pl.ds(i * size, size)
+            copies.append(pltpu.make_async_copy(src.at[rows], dst.at[rows], sems.at[k, i]))
+    for copy in copies:
+        copy.start()
+    for copy in copies:
+        copy.wait()
+
+
+def finish(arrays):
+    anywhere = pl.BlockSpec(memory_space=pl.ANY)
+    return pl.pallas_call(
+        finish_kernel,
+        out_shape=tuple(jax.ShapeDtypeStruct(a.shape, a.dtype) for a in arrays),
+        in_specs=[anywhere] * len(arrays),
+        out_specs=(anywhere,) * len(arrays),
+        scratch_shapes=[pltpu.SemaphoreType.DMA((len(arrays), 4))],
+    )(*arrays)
 
 
 def body(chips, ring, mixer_input, log_decay, b_rows, c_rows, skip_gain, grad_out):
@@ -400,10 +485,12 @@
     lb = width // 2 // LANES
     far = ring // 2
     vm = pltpu.VMEM
-    piece = (lb, chips, pr, LANES)
     msg = (chips, lb * pr, LANES)
     msg_l = (chips, lb * pr + 8, LANES)
     scratch = [
+        vm((length, width), BF16), vm((length, width), BF16),
+        vm((length, state_n), BF16), vm((length, state_n), BF16),
+        vm((length, width), BF16), vm((length, width), BF16),
         vm((nc, q, width), BF16), vm((nc, q, width), BF16),
         vm((nc, q, width), F32), vm((nc, q, width), F32),
         vm((nc, state_n, width), F32), vm((nc, state_n, width), F32),
@@ -414,17 +501,20 @@
         vm((2 * kh, width), BF16), vm((q, 2 * kh), BF16), vm((q, 2 * kh), BF16),
         vm((2 * nc, width), F32), vm((1, width), F32), vm((3 * q, q), BF16), vm((1, width), F32),
         vm((state_n, width), F32), vm((state_n, width), F32),
-        vm((2, *piece), F32), vm((2, *piece), F32), vm((2, 8, LANES), F32), vm((8, LANES), F32),
-        vm(piece, F32), vm(piece, F32),
+        vm((2, *msg), F32), vm((2, *msg), F32), vm((2, 8, LANES), F32), vm((8, LANES), F32),
+        vm(msg, F32), vm(msg, F32),
         vm(msg_l, F32), vm(msg, F32), vm(msg_l, F32), vm(msg, F32), vm(msg, F32), vm(msg, F32),
-        vm(msg, F32), vm(msg, F32), vm(piece, F32), vm(piece, F32), vm(piece, F32), vm(piece, F32),
+        vm(msg, F32), vm(msg, F32), vm(msg, F32), vm(msg, F32), vm(msg, F32), vm(msg, F32),
         vm((2, 2, far, q, state_n), F32),
-        pltpu.SemaphoreType.DMA((5,)), pltpu.SemaphoreType.DMA((5,)),
+        pltpu.SemaphoreType.DMA((2, nc + 1)), pltpu.SemaphoreType.DMA((2, nc)),
+        pltpu.SemaphoreType.DMA, pltpu.SemaphoreType.DMA,
+        pltpu.SemaphoreType.DMA((4, chips)), pltpu.SemaphoreType.DMA((4, chips)),
         pltpu.SemaphoreType.DMA((4, chips)), pltpu.SemaphoreType.DMA((4, chips)),
         pltpu.SemaphoreType.DMA((2, 2, far)), pltpu.SemaphoreType.DMA((2, 2, far)),
     ]
     whole = pl.BlockSpec(memory_space=pltpu.VMEM)
-    return pl.pallas_call(
+    anywhere = pl.BlockSpec(memory_space=pl.ANY)
+    return finish(pl.pallas_call(
         functools.partial(kernel, chips, ring),
         out_shape=(
             jax.ShapeDtypeStruct((length, width), BF16),
@@ -433,12 +523,12 @@
             jax.ShapeDtypeStruct((q, state_n), F32),
             jax.ShapeDtypeStruct((q, state_n), F32),
         ),
-        in_specs=[whole] * 6,
-        out_specs=(whole,) * 5,
+        in_specs=[anywhere, whole, anywhere, anywhere, whole, anywhere],
+        out_specs=(anywhere, anywhere, whole, whole, whole),
         scratch_shapes=scratch,
         compiler_params=pltpu.CompilerParams(
             collective_id=0, has_side_effects=True, vmem_limit_bytes=60 * 1024 * 1024),
-    )(mixer_input, log_decay, b_rows, c_rows, skip_gain.reshape(1, heads), grad_out)
+    )(mixer_input, log_decay, b_rows, c_rows, skip_gain.reshape(1, heads), grad_out))
 
 
 def solution(mesh):

time: 66.4 us -> 189 us (2.85)
  Pallas kernels: 58.3 us -> 188 us
  local copies, waits for them, and re-layouts: 6.45 us -> 0 us
    pallas_call x0 -> x1, Pallas kernels: none -> 134 us  [finish(): pl.pallas_call(finish_kernel, out_shape=tuple((jax.ShapeDtypeStruct(a.sha...]
    unnamed x13 -> x0, local copies, waits for them, and re-layouts: 6.45 us -> none
    pallas_call x1, Pallas kernels: 58.3 us -> 53.4 us  [body(): pl.pallas_call(functools.partial(kernel, chips, ring), out_shape=(jax.Sha...]
where the time goes in v2:
time: 189 us; the launch traced here: 188 us
  Pallas kernels  188 us (99%)
    pallas_call x1, Pallas kernels, finish(): pl.pallas_call(finish_kernel, out_shape=tuple((jax.ShapeDtypeStruct(a.sha...  134 us
    pallas_call x1, Pallas kernels, body(): pl.pallas_call(functools.partial(kernel, chips, ring), out_shape=(jax.Sha...  53.4 us

profile of v2, /device:TPU:8, one launch (start us, length us, event | category | flops | bytes accessed | tf_op | source)
XLA Modules:
  0.0 188.4 jit_solution(13414122351800264070)
XLA Ops:
  0.6 53.4 %shard_map.101 = (bf16[1024,1024]{1,0:T(8,128)(2,1)}, bf16[1024,1024]{1,0:T(8,128)(2,1)}, f32[16,1024]{1,0:T(8,128)}, f32[128,128]{1,0:T(8,128)}, f32[128,128]{1,0:T(8,128)}) custom-call(bf16[1024,1024]{1,0:T(8,128)(2,1)} %x_ref.1, f32[16,1024]{1,0:T(8,128)} %ld_ref.1, bf16[1024,128]{1,0:T(8,128)(2,1)} %b_any.1, bf16[1024,128]{1,0:T(8,128)(2,1)} %c_any.1, ...), custom_call_target="tpu_custom_call" | custom-call | tf_op jit(solution)/shard_map/pallas_call | solution.py:517
  54.1 134.3 %shard_map.102 = (bf16[1024,1024]{1,0:T(8,128)(2,1)}, bf16[1024,1024]{1,0:T(8,128)(2,1)}, f32[16,1024]{1,0:T(8,128)}, f32[128,128]{1,0:T(8,128)}, f32[128,128]{1,0:T(8,128)}) custom-call(bf16[1024,1024]{1,0:T(8,128)(2,1)} %get-tuple-element.10.refs_0_, bf16[1024,1024]{1,0:T(8,128)(2,1)} %get-tuple-element.11.refs_1_, f32[16,1024]{1,0:T(8,128)} %get-tuple-element.12.refs_2_, ...), custom_call_target="tpu_custom_call" | custom-call | tf_op jit(solution)/shard_map/pallas_call | solution.py:468

commit v3 on v2

--- a/solution.py
+++ b/solution.py
@@ -43,14 +43,14 @@
     return jnp.concatenate(out, axis=axis)
 
 
-def kernel(chips, ring, x_ref, ld_ref, b_any, c_any, skip_ref, dy_ref,
+def kernel(chips, ring, x_ref, ld_any, b_any, c_any, skip_any, dy_ref,
            y_ref, dx_ref, gld_ref, gb_ref, gc_ref,
-           xv, dyv, b_ref, c_ref, yv, dxv,
+           xv, dyv, b_ref, c_ref, ld_ref, skip_ref,
            xs, ds, a_exp, inv_exp, gmat, hmat, sp, tp, mm, mt, dcs, dbs, bnd,
            spread, parts_a, parts_i, rows, lam, tri_s, skipe,
            state, grad, th, tb, lamh, lamp, pf, pb, cmf, cmb, rf, rb, esf, esb,
            ref_, reb, p2f, p2b, pef, peb, rsbuf,
-           in_s, out_s, lam_s, lam_r, pair_s, pair_r, a2a_s, a2a_r, rs_s, rs_r):
+           in_s, lam_s, lam_r, pair_s, pair_r, a2a_s, a2a_r, rs_s, rs_r):
     seq = lax.axis_index("seq")
     z = lax.axis_index("exp")
     core = lax.rem(seq, 2)
@@ -108,15 +108,18 @@
         return pltpu.make_async_copy(src.at[rows_of(c)], dst.at[rows_of(c)], in_s.at[k, c])
 
     def whole_load(k):
-        return pltpu.make_async_copy((b_any, c_any)[k], (b_ref, c_ref)[k], in_s.at[k, nc])
-
-    whole_load(0).start()
+        src, dst = ((b_any, b_ref), (c_any, c_ref), (ld_any, ld_ref), (skip_any, skip_ref))[k]
+        return pltpu.make_async_copy(src, dst, in_s.at[k % 2, nc + k // 2])
+
+    for k in (2, 3, 0):
+        whole_load(k).start()
     for c in range(nc):
         loads(0, x_ref, xv, c).start()
     whole_load(1).start()
     for c in reversed(range(nc)):
         loads(1, dy_ref, dyv, c).start()
 
+    whole_load(2).wait()
     stacked = jnp.concatenate([ld_ref[:, c * q:(c + 1) * q] for c in range(nc)], axis=0)
     tri = (iota((q, q), 0) >= iota((q, q), 1)).astype(BF16)
     cum = nt(jnp.concatenate([tri] * 3, axis=1), pieces(stacked, 3, 1))
@@ -141,6 +144,7 @@
         for r in range(lb):
             lamh[h, r:r + 1, :] = total[:, h * half + r * LANES:h * half + (r + 1) * LANES]
     head_one = (iota((heads, width), 1) // HEAD == iota((heads, width), 0)).astype(BF16)
+    whole_load(3).wait()
     skipe[...] = nn(pieces(skip_ref[...], 3, 1), jnp.concatenate([head_one] * 3, axis=0))
 
     lane_chunk = lax.rem(iota((q, 2 * kh), 1), kh) // heads
@@ -403,10 +407,6 @@
 
     last_row = iota((q, width), 0) == q - 1
 
-    def stores(k, c):
-        src, dst = ((yv, y_ref), (dxv, dx_ref))[k]
-        return pltpu.make_async_copy(src.at[rows_of(c)], dst.at[rows_of(c)], out_s.at[k, c])
-
     def outputs(c, _):
         x_c, d_c = xs[c], ds[c]
         acc_y = nn(jnp.concatenate([mm[c], c_ref[rows_of(c), :]], axis=1),
@@ -414,16 +414,14 @@
         acc_x = nn(jnp.concatenate([mt[c], b_ref[rows_of(c), :]], axis=1),
                    jnp.concatenate([d_c, tp[c]], axis=0))
         gain = skipe[...]
-        yv[rows_of(c), :] = (a_exp[c] * acc_y + gain * xv[rows_of(c), :].astype(F32)).astype(BF16)
-        dxv[rows_of(c), :] = (inv_exp[c] * acc_x + gain * dyv[rows_of(c), :].astype(F32)).astype(BF16)
+        y_ref[rows_of(c), :] = (a_exp[c] * acc_y + gain * xv[rows_of(c), :].astype(F32)).astype(BF16)
+        dx_ref[rows_of(c), :] = (inv_exp[c] * acc_x + gain * dyv[rows_of(c), :].astype(F32)).astype(BF16)
         diff = d_c.astype(F32) * acc_y - x_c.astype(F32) * acc_x
         diff = diff + jnp.where(last_row, bnd[pl.ds(c, 1), :], 0.0)
         hi = diff.astype(BF16)
         lo = (diff - hi.astype(F32)).astype(BF16)
         per_head = nt(head_one, hi) + nt(head_one, lo)
         gld_ref[:, rows_of(c)] = nn(pieces(per_head, 3, 1), tri_s[...])
-        stores(0, c).start()
-        stores(1, c).start()
         return 0
 
     done = 0
@@ -438,9 +436,6 @@
     rs_end(0, dcs, gc_ref)
     rs_end(1, dbs, gb_ref)
 
-    for c in range(nc):
-        stores(0, c).wait()
-        stores(1, c).wait()
     for copy in [send_lam, *pair_f, *pair_b, *go_f, *go_b, *ret_f, *ret_b,
                  *[c for _, c in send_2f], *[c for _, c in send_2b], *started.values()]:
         copy.wait_send()
@@ -464,13 +459,13 @@
 
 
 def finish(arrays):
-    anywhere = pl.BlockSpec(memory_space=pl.ANY)
     return pl.pallas_call(
         finish_kernel,
         out_shape=tuple(jax.ShapeDtypeStruct(a.shape, a.dtype) for a in arrays),
-        in_specs=[anywhere] * len(arrays),
-        out_specs=(anywhere,) * len(arrays),
+        in_specs=[pl.BlockSpec(memory_space=pltpu.VMEM)] * len(arrays),
+        out_specs=(pl.BlockSpec(memory_space=pl.ANY),) * len(arrays),
         scratch_shapes=[pltpu.SemaphoreType.DMA((len(arrays), 4))],
+        compiler_params=pltpu.CompilerParams(vmem_limit_bytes=16 * 1024 * 1024),
     )(*arrays)
 
 
@@ -490,7 +485,7 @@
     scratch = [
         vm((length, width), BF16), vm((length, width), BF16),
         vm((length, state_n), BF16), vm((length, state_n), BF16),
-        vm((length, width), BF16), vm((length, width), BF16),
+        vm((heads, length), F32), vm((1, heads), F32),
         vm((nc, q, width), BF16), vm((nc, q, width), BF16),
         vm((nc, q, width), F32), vm((nc, q, width), F32),
         vm((nc, state_n, width), F32), vm((nc, state_n, width), F32),
@@ -506,29 +501,30 @@
         vm(msg_l, F32), vm(msg, F32), vm(msg_l, F32), vm(msg, F32), vm(msg, F32), vm(msg, F32),
         vm(msg, F32), vm(msg, F32), vm(msg, F32), vm(msg, F32), vm(msg, F32), vm(msg, F32),
         vm((2, 2, far, q, state_n), F32),
-        pltpu.SemaphoreType.DMA((2, nc + 1)), pltpu.SemaphoreType.DMA((2, nc)),
+        pltpu.SemaphoreType.DMA((2, nc + 2)),
         pltpu.SemaphoreType.DMA, pltpu.SemaphoreType.DMA,
         pltpu.SemaphoreType.DMA((4, chips)), pltpu.SemaphoreType.DMA((4, chips)),
         pltpu.SemaphoreType.DMA((4, chips)), pltpu.SemaphoreType.DMA((4, chips)),
         pltpu.SemaphoreType.DMA((2, 2, far)), pltpu.SemaphoreType.DMA((2, 2, far)),
     ]
     whole = pl.BlockSpec(memory_space=pltpu.VMEM)
-    anywhere = pl.BlockSpec(memory_space=pl.ANY)
+    outside = pl.BlockSpec(memory_space=pltpu.HBM)
     return finish(pl.pallas_call(
         functools.partial(kernel, chips, ring),
         out_shape=(
-            jax.ShapeDtypeStruct((length, width), BF16),
-            jax.ShapeDtypeStruct((length, width), BF16),
-            jax.ShapeDtypeStruct((heads, length), F32),
-            jax.ShapeDtypeStruct((q, state_n), F32),
-            jax.ShapeDtypeStruct((q, state_n), F32),
+            vm((length, width), BF16),
+            vm((length, width), BF16),
+            vm((heads, length), F32),
+            vm((q, state_n), F32),
+            vm((q, state_n), F32),
         ),
-        in_specs=[anywhere, whole, anywhere, anywhere, whole, anywhere],
-        out_specs=(anywhere, anywhere, whole, whole, whole),
+        in_specs=[outside] * 6,
+        out_specs=(whole,) * 5,
         scratch_shapes=scratch,
         compiler_params=pltpu.CompilerParams(
-            collective_id=0, has_side_effects=True, vmem_limit_bytes=60 * 1024 * 1024),
-    )(mixer_input, log_decay, b_rows, c_rows, skip_gain.reshape(1, heads), grad_out))
+            collective_id=0, has_side_effects=True, vmem_limit_bytes=48 * 1024 * 1024),
+    )(*[pltpu.with_memory_space_constraint(a, pltpu.HBM) for a in (
+        mixer_input, log_decay, b_rows, c_rows, skip_gain.reshape(1, heads), grad_out)]))
 
 
 def solution(mesh):

time: 189 us -> 55.5 us (0.29)
  Pallas kernels: 188 us -> 54.7 us
    pallas_call x1, Pallas kernels: 134 us -> 2.23 us  [finish(): pl.pallas_call(finish_kernel, out_shape=tuple((jax.ShapeDtypeStruct(a.sha...]
where the time goes in v3:
time: 55.5 us; the launch traced here: 55.3 us
  Pallas kernels  54.7 us (99%)
  between operations  0.64 us (1%)
    pallas_call x1, Pallas kernels, body(): pl.pallas_call(functools.partial(kernel, chips, ring), out_shape=(vm((len...  52.4 us
    pallas_call x1, Pallas kernels, finish(): pl.pallas_call(finish_kernel, out_shape=tuple((jax.ShapeDtypeStruct(a.sha...  2.23 us

profile of v3, /device:TPU:8, one launch (start us, length us, event | category | flops | bytes accessed | tf_op | source)
XLA Modules:
  0.0 55.3 jit_solution(10784362407837747222)
XLA Ops:
  0.6 52.4 %shard_map.101 = (bf16[1024,1024]{1,0:T(8,128)(2,1)S(1)}, bf16[1024,1024]{1,0:T(8,128)(2,1)S(1)}, f32[16,1024]{1,0:T(8,128)S(1)}, f32[128,128]{1,0:T(8,128)S(1)}, f32[128,128]{1,0:T(8,128)S(1)}) custom-call(bf16[1024,1024]{1,0:T(8,128)(2,1)} %x_ref.1, f32[16,1024]{1,0:T(8,128)} %ld_any.1, bf16[1024,128]{1,0:T(8,128)(2,1)} %b_any.1, bf16[1024,128]{1,0:T(8,128)(2,1)} %c_any.1, ...), custom_call_target="tpu_custom_call" | custom-call | tf_op jit(solution)/shard_map/pallas_call | solution.py:512
  53.1 2.2 %shard_map.102 = (bf16[1024,1024]{1,0:T(8,128)(2,1)}, bf16[1024,1024]{1,0:T(8,128)(2,1)}, f32[16,1024]{1,0:T(8,128)}, f32[128,128]{1,0:T(8,128)}, f32[128,128]{1,0:T(8,128)}) custom-call(bf16[1024,1024]{1,0:T(8,128)(2,1)S(1)} %get-tuple-element.10.refs_0_, bf16[1024,1024]{1,0:T(8,128)(2,1)S(1)} %get-tuple-element.11.refs_1_, ...), custom_call_target="tpu_custom_call" | custom-call | tf_op jit(solution)/shard_map/pallas_call | solution.py:462

commit v4 on v3

--- a/solution.py
+++ b/solution.py
@@ -47,7 +47,7 @@
            y_ref, dx_ref, gld_ref, gb_ref, gc_ref,
            xv, dyv, b_ref, c_ref, ld_ref, skip_ref,
            xs, ds, a_exp, inv_exp, gmat, hmat, sp, tp, mm, mt, dcs, dbs, bnd,
-           spread, parts_a, parts_i, rows, lam, tri_s, skipe,
+           spread, parts_a, parts_i, rows, heads_of, tri_s, skipe,
            state, grad, th, tb, lamh, lamp, pf, pb, cmf, cmb, rf, rb, esf, esb,
            ref_, reb, p2f, p2b, pef, peb, rsbuf,
            in_s, lam_s, lam_r, pair_s, pair_r, a2a_s, a2a_r, rs_s, rs_r):
@@ -87,6 +87,33 @@
         dy, dx = offsets[d]
         return lax.rem(cy + ny - dy, ny) * nx + lax.rem(cx + nx - dx, nx)
 
+    def remote(src, dst, s_sem, r_sem, dev):
+        return pltpu.make_async_remote_copy(
+            src_ref=src, dst_ref=dst, send_sem=s_sem, recv_sem=r_sem,
+            device_id=dev, device_id_type=MESH)
+
+    def rows_of(c):
+        return pl.ds(pl.multiple_of(c * q, q), q)
+
+    quart = length // 4
+
+    def loads(k, part):
+        src, dst = ((x_ref, xv), (dy_ref, dyv))[k]
+        span = pl.ds(part * quart, quart)
+        return pltpu.make_async_copy(src.at[span], dst.at[span], in_s.at[k, part])
+
+    def whole_load(k):
+        src, dst = ((b_any, b_ref), (c_any, c_ref), (ld_any, ld_ref), (skip_any, skip_ref))[k]
+        return pltpu.make_async_copy(src, dst, in_s.at[k % 2, 4 + k // 2])
+
+    whole_load(2).start()
+    for part in range(4):
+        loads(0, part).start()
+    for k in (0, 1, 3):
+        whole_load(k).start()
+    for part in range(4):
+        loads(1, part).start()
+
     barrier = pltpu.get_barrier_semaphore()
     pl.semaphore_signal(barrier, inc=1, device_id=partner, device_id_type=MESH)
     for d in range(count):
@@ -96,42 +123,32 @@
     pl.semaphore_signal(barrier, inc=1, device_id=(seq, z_dn), device_id_type=MESH)
     pl.semaphore_signal(barrier, inc=1, device_id=(seq, z_up), device_id_type=MESH)
 
-    def remote(src, dst, s_sem, r_sem, dev):
-        return pltpu.make_async_remote_copy(
-            src_ref=src, dst_ref=dst, send_sem=s_sem, recv_sem=r_sem,
-            device_id=dev, device_id_type=MESH)
-
-    def rows_of(c):
-        return pl.ds(pl.multiple_of(c * q, q), q)
-
-    def loads(k, src, dst, c):
-        return pltpu.make_async_copy(src.at[rows_of(c)], dst.at[rows_of(c)], in_s.at[k, c])
-
-    def whole_load(k):
-        src, dst = ((b_any, b_ref), (c_any, c_ref), (ld_any, ld_ref), (skip_any, skip_ref))[k]
-        return pltpu.make_async_copy(src, dst, in_s.at[k % 2, nc + k // 2])
-
-    for k in (2, 3, 0):
-        whole_load(k).start()
-    for c in range(nc):
-        loads(0, x_ref, xv, c).start()
-    whole_load(1).start()
-    for c in reversed(range(nc)):
-        loads(1, dy_ref, dyv, c).start()
+    def head_of(shape, axis):
+        return lax.shift_right_logical(iota(shape, axis), HEAD.bit_length() - 1)
+
+    lane_heads = heads.bit_length() - 1
+    one = ((iota((kh, width), 0) & (heads - 1)) == head_of((kh, width), 1)).astype(BF16)
+    spread[0:kh, :] = one
+    spread[kh:2 * kh, :] = one
+    tri = (iota((q, q), 0) >= iota((q, q), 1)).astype(BF16)
+    tri3 = jnp.concatenate([tri] * 3, axis=1)
+    own_row = lax.shift_right_logical(iota((nc, kh), 1), lane_heads) == iota((nc, kh), 0)
+    lane_chunk = lax.shift_right_logical(iota((q, 2 * kh), 1) & (kh - 1), lane_heads)
 
     whole_load(2).wait()
     stacked = jnp.concatenate([ld_ref[:, c * q:(c + 1) * q] for c in range(nc)], axis=0)
-    tri = (iota((q, q), 0) >= iota((q, q), 1)).astype(BF16)
-    cum = nt(jnp.concatenate([tri] * 3, axis=1), pieces(stacked, 3, 1))
-    tri_s[...] = jnp.concatenate([tri] * 3, axis=0)
+    cum = nt(tri3, pieces(stacked, 3, 1))
     rho = cum[q // 2 - 1:q // 2, :]
     tot = cum[q - 1:q, :]
     shifted = cum - rho
+    parts_i[...] = pieces(jnp.exp(-shifted), 2, 1)
     parts_a[...] = pieces(jnp.exp(shifted), 2, 1)
-    parts_i[...] = pieces(jnp.exp(-shifted), 2, 1)
-    one = (lax.rem(iota((kh, width), 0), heads) == iota((kh, width), 1) // HEAD).astype(BF16)
-    spread[...] = jnp.concatenate([one, one], axis=0)
-    own_row = iota((nc, kh), 1) // heads == iota((nc, kh), 0)
+
+    def by_chunk(parts):
+        return jnp.concatenate(
+            [jnp.where(lane_chunk == c, parts[...], jnp.zeros((), BF16)) for c in range(nc)], axis=0)
+
+    inv_exp[...] = nn(by_chunk(parts_i), spread[...])
     pair_rows = jnp.concatenate(
         [jnp.where(own_row, jnp.exp(rho), 0.0), jnp.where(own_row, jnp.exp(tot - rho), 0.0)], axis=0)
     rows[...] = nn(pieces(pair_rows, 3, 1), jnp.concatenate([one, one, one], axis=0))
@@ -139,45 +156,33 @@
     total = both[0:1, :]
     for c in range(1, nc):
         total = total * both[c:c + 1, :]
-    lam[...] = total
     for h in range(2):
         for r in range(lb):
             lamh[h, r:r + 1, :] = total[:, h * half + r * LANES:h * half + (r + 1) * LANES]
-    head_one = (iota((heads, width), 1) // HEAD == iota((heads, width), 0)).astype(BF16)
-    whole_load(3).wait()
-    skipe[...] = nn(pieces(skip_ref[...], 3, 1), jnp.concatenate([head_one] * 3, axis=0))
-
-    lane_chunk = lax.rem(iota((q, 2 * kh), 1), kh) // heads
-
-    state[...] = jnp.zeros_like(state)
-    grad[...] = jnp.zeros_like(grad)
-
-    def fwd_local(c, _):
-        inv = nn(jnp.where(lane_chunk == c, parts_i[...], jnp.zeros((), BF16)), spread[...])
-        inv_exp[c] = inv
-        loads(0, x_ref, xv, c).wait()
-        scaled = (xv[rows_of(c), :].astype(F32) * inv).astype(BF16)
+
+    def fwd_local(c):
+        if c % (nc // 4) == 0:
+            loads(0, c // (nc // 4)).wait()
+        rc = slice(c * q, (c + 1) * q)
+        scaled = (xv[rc, :].astype(F32) * inv_exp[rc, :]).astype(BF16)
         xs[c] = scaled
-        got = tn(b_ref[rows_of(c), :], scaled)
+        got = tn(b_ref[rc, :], scaled)
         gmat[c] = got
-        f = rows[pl.ds(c, 1), :]
-        g = rows[pl.ds(nc + c, 1), :]
-        state[...] = g * (f * state[...] + got)
-        return 0
-
-    def bwd_local(i, _):
-        c = nc - 1 - i
-        a = nn(jnp.where(lane_chunk == c, parts_a[...], jnp.zeros((), BF16)), spread[...])
-        a_exp[c] = a
-        loads(1, dy_ref, dyv, c).wait()
-        scaled = (dyv[rows_of(c), :].astype(F32) * a).astype(BF16)
+        f = rows[c:c + 1, :]
+        g = rows[nc + c:nc + c + 1, :]
+        state[...] = g * got if c == 0 else g * (f * state[...] + got)
+
+    def bwd_local(c):
+        if (c + 1) % (nc // 4) == 0:
+            loads(1, c // (nc // 4)).wait()
+        rc = slice(c * q, (c + 1) * q)
+        scaled = (dyv[rc, :].astype(F32) * a_exp[rc, :]).astype(BF16)
         ds[c] = scaled
-        got = tn(c_ref[rows_of(c), :], scaled)
+        got = tn(c_ref[rc, :], scaled)
         hmat[c] = got
-        f = rows[pl.ds(c, 1), :]
-        g = rows[pl.ds(nc + c, 1), :]
-        grad[...] = f * (g * grad[...] + got)
-        return 0
+        f = rows[c:c + 1, :]
+        g = rows[nc + c:nc + c + 1, :]
+        grad[...] = f * got if c == nc - 1 else f * (g * grad[...] + got)
 
     def to_halves(src, dst):
         for h in range(2):
@@ -283,159 +288,161 @@
     lower = iota((q, q), 0) >= iota((q, q), 1)
     upper = iota((q, q), 0) <= iota((q, q), 1)
 
-    def inner(c, _):
-        bb, cc = b_ref[rows_of(c), :], c_ref[rows_of(c), :]
+    def inner(c):
+        rc = slice(c * q, (c + 1) * q)
+        bb, cc = b_ref[rc, :], c_ref[rc, :]
         mm[c] = jnp.where(lower, nt(cc, bb), 0.0).astype(BF16)
         mt[c] = jnp.where(upper, nt(bb, cc), 0.0).astype(BF16)
         dm = jnp.where(lower, nt(ds[c], xs[c]), 0.0).astype(BF16)
         dcs[c] = nn(dm, bb)
         dbs[c] = tn(dm, cc)
-        return 0
 
     whole_load(0).wait()
-    lax.fori_loop(0, nc, fwd_local, 0)
+    for c in range(nc):
+        fwd_local(c)
     to_halves(state, th)
     pl.semaphore_wait(barrier, chips + 2)
     send_lam = remote(lamh.at[other], lamp, lam_s, lam_r, partner)
     send_lam.start()
     pair_f = pair_send(0, th.at[other], pf, piece_of)
     whole_load(1).wait()
-    lax.fori_loop(0, nc // 2, bwd_local, 0)
+    a_exp[...] = nn(by_chunk(parts_a), spread[...])
+    for c in reversed(range(nc // 2, nc)):
+        bwd_local(c)
     send_lam.wait_recv()
     go_f = combine(0, pair_f, th, pf, cmf, rf, True)
-    lax.fori_loop(nc // 2, nc, bwd_local, 0)
+    for c in reversed(range(nc // 2)):
+        bwd_local(c)
     to_halves(grad, tb)
     pair_b = pair_send(1, tb.at[other], pb, piece_of)
-    lax.fori_loop(0, nc // 4, inner, 0)
+    whole_load(3).wait()
+    for c in range(nc // 4):
+        inner(c)
     go_b = combine(1, pair_b, tb, pb, cmb, rb, False)
-    lax.fori_loop(nc // 4, nc // 2, inner, 0)
+    for c in range(nc // 4, nc // 2):
+        inner(c)
     ret_f = scan_pieces(go_f, 2, rf, esf, ref_, range(chips))
-    lax.fori_loop(nc // 2, 3 * nc // 4, inner, 0)
+    for c in range(nc // 2, 3 * nc // 4):
+        inner(c)
     ret_b = scan_pieces(go_b, 3, rb, esb, reb, list(reversed(range(chips))))
-    lax.fori_loop(3 * nc // 4, nc, inner, 0)
+    for c in range(3 * nc // 4, nc):
+        inner(c)
+    tri_s[...] = jnp.concatenate([tri] * 3, axis=0)
+    head_one = (head_of((heads, width), 1) == iota((heads, width), 0)).astype(BF16)
+    skipe[...] = nn(pieces(skip_ref[...], 3, 1), jnp.concatenate([head_one] * 3, axis=0))
+    col = (head_of((width, heads), 0) == iota((width, heads), 1)).astype(BF16)
+    heads_of[...] = jnp.concatenate([col, col], axis=0)
     send_2f = hand_out(2, ret_f, ref_, th, pf, p2f, pef, state, True)
     take_in(send_2f, pef, state)
 
-    def fwd_state(c, _):
-        f = rows[pl.ds(c, 1), :]
-        g = rows[pl.ds(nc + c, 1), :]
-        entering = f * state[...]
+    for c in range(nc):
+        entering = rows[c:c + 1, :] * state[...]
         sp[c] = entering.astype(BF16)
         leaving = entering + gmat[c]
         gmat[c] = leaving
-        state[...] = g * leaving
-        return 0
-
-    lax.fori_loop(0, nc, fwd_state, 0)
+        state[...] = rows[nc + c:nc + c + 1, :] * leaving
 
     hq = q // 2
-
-    def rs_copy(t, way, step, src):
-        to = (seq, z_dn if way == 0 else z_up)
-        dst = rsbuf.at[t, way, step]
-        if step == 0:
-            dst = dst.at[pl.ds(way * hq, hq)]
-        return remote(src, dst, rs_s.at[t, way, step], rs_r.at[t, way, step], to)
+    started = {}
 
     def chunk_at(way, step):
         gap = far - step
         return lax.rem(z + (ring - gap if way == 0 else gap), ring)
 
-    started = {}
-
-    def rs_start(t, own):
+    def rs_send(t, own, way, step, long):
+        lo = (way if long else 1 - way) * hq
+        first_step = 0 if long else 1
+        k = chunk_at(way, step)
+        if step == first_step:
+            src = own.at[k, pl.ds(lo, hq)]
+        else:
+            started[t, way, step - 1, long].wait_recv()
+            rsbuf[t, way, step - 1, lo:lo + hq, :] += own[k, lo:lo + hq, :]
+            src = rsbuf.at[t, way, step - 1, pl.ds(lo, hq)]
+        copy = remote(src, rsbuf.at[t, way, step, pl.ds(lo, hq)],
+                      rs_s.at[t, way, step, int(long)], rs_r.at[t, way, step, int(long)],
+                      (seq, z_dn if way == 0 else z_up))
+        copy.start()
+        started[t, way, step, long] = copy
+
+    def rs_poll(t, own, step):
         for way in range(2):
-            src = own.at[chunk_at(way, 0), pl.ds(way * hq, hq)]
-            started[t, way, 0] = rs_copy(t, way, 0, src)
-            started[t, way, 0].start()
-
-    def rs_next(t, own, step):
-        for way in range(2):
-            started[t, way, step - 1].wait_recv()
-            k = chunk_at(way, step)
-            if step == 1:
-                lo = way * hq
-                rsbuf[t, way, 0, lo:lo + hq, :] += own[k, lo:lo + hq, :]
-                lo = hq - lo
-                rsbuf[t, way, 0, lo:lo + hq, :] = own[k, lo:lo + hq, :]
-            else:
-                rsbuf[t, way, step - 1] += own[k]
-            started[t, way, step] = rs_copy(t, way, step, rsbuf.at[t, way, step - 1])
-            started[t, way, step].start()
+            rs_send(t, own, way, step, True)
+        if step + 1 < far:
+            for way in range(2):
+                rs_send(t, own, way, step + 1, False)
 
     def rs_end(t, own, out):
         for way in range(2):
-            started[t, way, far - 1].wait_recv()
-        last = rsbuf[t, 0, far - 1] + rsbuf[t, 1, far - 1]
-        if far == 1:
-            raise ValueError("ring")
-        out[...] = own[z] + last
-
-    def dc_chunk(i, _):
-        c = lax.rem(z + far + i, ring)
+            for long in (False, True):
+                started[t, way, far - 1, long].wait_recv()
+        out[...] = own[z] + rsbuf[t, 0, far - 1] + rsbuf[t, 1, far - 1]
+
+    def near(i):
+        gap = far - (i + 1) // 2
+        return lax.rem(z + (gap if i % 2 == 1 else ring - gap), ring)
+
+    def dc_chunk(i):
+        c = near(i)
         dcs[c] += nt(ds[c], sp[c])
-        return 0
-
-    def db_chunk(i, _):
-        c = lax.rem(z + far + i, ring)
+
+    def db_chunk(i):
+        c = near(i)
         dbs[c] += nt(xs[c], tp[c])
-        return 0
-
-    dc_chunk(0, 0)
-    rs_start(0, dcs)
-    lax.fori_loop(1, nc, dc_chunk, 0)
-
+
+    for i in range(3):
+        dc_chunk(i)
+    rs_poll(0, dcs, 0)
     send_2b = hand_out(3, ret_b, reb, tb, pb, p2b, peb, grad, False)
+    for i in range(3, nc):
+        dc_chunk(i)
+    rs_poll(0, dcs, 1)
     take_in(send_2b, peb, grad)
 
-    def bwd_state(i, _):
-        c = nc - 1 - i
-        f = rows[pl.ds(c, 1), :]
-        g = rows[pl.ds(nc + c, 1), :]
-        later = g * grad[...]
+    for c in reversed(range(nc)):
+        later = rows[nc + c:nc + c + 1, :] * grad[...]
         low = later.astype(BF16)
         tp[c] = low
-        bnd[pl.ds(c, 1), :] = jnp.sum(low.astype(F32) * gmat[c], axis=0, keepdims=True)
-        grad[...] = f * (later + hmat[c])
-        return 0
-
-    lax.fori_loop(0, nc, bwd_state, 0)
-    rs_next(0, dcs, 1)
-    db_chunk(0, 0)
-    rs_start(1, dbs)
-    lax.fori_loop(1, nc, db_chunk, 0)
+        bnd[c:c + 1, :] = jnp.sum(low.astype(F32) * gmat[c], axis=0, keepdims=True)
+        if c:
+            grad[...] = rows[c:c + 1, :] * (later + hmat[c])
+    for i in range(3):
+        db_chunk(i)
+    rs_poll(1, dbs, 0)
+    rs_poll(0, dcs, 2) if far > 2 else None
+    for i in range(3, nc):
+        db_chunk(i)
 
     last_row = iota((q, width), 0) == q - 1
 
-    def outputs(c, _):
+    def outputs(c):
+        rc = slice(c * q, (c + 1) * q)
         x_c, d_c = xs[c], ds[c]
-        acc_y = nn(jnp.concatenate([mm[c], c_ref[rows_of(c), :]], axis=1),
+        acc_y = nn(jnp.concatenate([mm[c], c_ref[rc, :]], axis=1),
                    jnp.concatenate([x_c, sp[c]], axis=0))
-        acc_x = nn(jnp.concatenate([mt[c], b_ref[rows_of(c), :]], axis=1),
+        acc_x = nn(jnp.concatenate([mt[c], b_ref[rc, :]], axis=1),
                    jnp.concatenate([d_c, tp[c]], axis=0))
         gain = skipe[...]
-        y_ref[rows_of(c), :] = (a_exp[c] * acc_y + gain * xv[rows_of(c), :].astype(F32)).astype(BF16)
-        dx_ref[rows_of(c), :] = (inv_exp[c] * acc_x + gain * dyv[rows_of(c), :].astype(F32)).astype(BF16)
+        y_ref[rc, :] = (a_exp[rc, :] * acc_y + gain * xv[rc, :].astype(F32)).astype(BF16)
+        dx_ref[rc, :] = (inv_exp[rc, :] * acc_x + gain * dyv[rc, :].astype(F32)).astype(BF16)
         diff = d_c.astype(F32) * acc_y - x_c.astype(F32) * acc_x
-        diff = diff + jnp.where(last_row, bnd[pl.ds(c, 1), :], 0.0)
-        hi = diff.astype(BF16)
-        lo = (diff - hi.astype(F32)).astype(BF16)
-        per_head = nt(head_one, hi) + nt(head_one, lo)
-        gld_ref[:, rows_of(c)] = nn(pieces(per_head, 3, 1), tri_s[...])
-        return 0
+        diff = diff + jnp.where(last_row, bnd[c:c + 1, :], 0.0)
+        per_head = nn(pieces(diff, 2, 1), heads_of[...])
+        gld_ref[:, rc] = tn(pieces(per_head, 3, 0), tri_s[...])
 
     done = 0
     for step in range(1, far):
         upto = nc * step // far
-        lax.fori_loop(done, upto, outputs, 0)
+        for c in range(done, upto):
+            outputs(c)
         done = upto
-        if step + 1 < far:
-            rs_next(0, dcs, step + 1)
-        rs_next(1, dbs, step)
-    lax.fori_loop(done, nc, outputs, 0)
+        if 2 < step + 2 < far:
+            rs_poll(0, dcs, step + 2)
+        rs_poll(1, dbs, step)
+    for c in range(done, nc):
+        outputs(c)
     rs_end(0, dcs, gc_ref)
     rs_end(1, dbs, gb_ref)
-
     for copy in [send_lam, *pair_f, *pair_b, *go_f, *go_b, *ret_f, *ret_b,
                  *[c for _, c in send_2f], *[c for _, c in send_2b], *started.values()]:
         copy.wait_send()
@@ -487,25 +494,25 @@
         vm((length, state_n), BF16), vm((length, state_n), BF16),
         vm((heads, length), F32), vm((1, heads), F32),
         vm((nc, q, width), BF16), vm((nc, q, width), BF16),
-        vm((nc, q, width), F32), vm((nc, q, width), F32),
+        vm((length, width), F32), vm((length, width), F32),
         vm((nc, state_n, width), F32), vm((nc, state_n, width), F32),
         vm((nc, state_n, width), BF16), vm((nc, state_n, width), BF16),
         vm((nc, q, q), BF16), vm((nc, q, q), BF16),
         vm((nc, q, state_n), F32), vm((nc, q, state_n), F32),
         vm((nc, width), F32),
         vm((2 * kh, width), BF16), vm((q, 2 * kh), BF16), vm((q, 2 * kh), BF16),
-        vm((2 * nc, width), F32), vm((1, width), F32), vm((3 * q, q), BF16), vm((1, width), F32),
+        vm((2 * nc, width), F32), vm((2 * width, heads), BF16), vm((3 * q, q), BF16), vm((1, width), F32),
         vm((state_n, width), F32), vm((state_n, width), F32),
         vm((2, *msg), F32), vm((2, *msg), F32), vm((2, 8, LANES), F32), vm((8, LANES), F32),
         vm(msg, F32), vm(msg, F32),
         vm(msg_l, F32), vm(msg, F32), vm(msg_l, F32), vm(msg, F32), vm(msg, F32), vm(msg, F32),
         vm(msg, F32), vm(msg, F32), vm(msg, F32), vm(msg, F32), vm(msg, F32), vm(msg, F32),
         vm((2, 2, far, q, state_n), F32),
-        pltpu.SemaphoreType.DMA((2, nc + 2)),
+        pltpu.SemaphoreType.DMA((2, 6)),
         pltpu.SemaphoreType.DMA, pltpu.SemaphoreType.DMA,
         pltpu.SemaphoreType.DMA((4, chips)), pltpu.SemaphoreType.DMA((4, chips)),
         pltpu.SemaphoreType.DMA((4, chips)), pltpu.SemaphoreType.DMA((4, chips)),
-        pltpu.SemaphoreType.DMA((2, 2, far)), pltpu.SemaphoreType.DMA((2, 2, far)),
+        pltpu.SemaphoreType.DMA((2, 2, far, 2)), pltpu.SemaphoreType.DMA((2, 2, far, 2)),
     ]
     whole = pl.BlockSpec(memory_space=pltpu.VMEM)
     outside = pl.BlockSpec(memory_space=pltpu.HBM)

time: 55.5 us -> 55.4 us (level)
  no operation moved by 1% of the time
where the time goes in v4:
time: 55.4 us
  Pallas kernels  54.6 us (99%)
  between operations  0.8 us (1%)
    pallas_call x1, Pallas kernels, body(): pl.pallas_call(functools.partial(kernel, chips, ring), out_shape=(vm((len...  52.3 us
    pallas_call x1, Pallas kernels, finish(): pl.pallas_call(finish_kernel, out_shape=tuple((jax.ShapeDtypeStruct(a.sha...  2.23 us

profile of v4, /device:TPU:8, one launch (start us, length us, event | category | flops | bytes accessed | tf_op | source)
XLA Modules:
  0.0 55.4 jit_solution(993293035536091167)
XLA Ops:
  0.6 52.3 %shard_map.101 = (bf16[1024,1024]{1,0:T(8,128)(2,1)S(1)}, bf16[1024,1024]{1,0:T(8,128)(2,1)S(1)}, f32[16,1024]{1,0:T(8,128)S(1)}, f32[128,128]{1,0:T(8,128)S(1)}, f32[128,128]{1,0:T(8,128)S(1)}) custom-call(bf16[1024,1024]{1,0:T(8,128)(2,1)} %x_ref.1, f32[16,1024]{1,0:T(8,128)} %ld_any.1, bf16[1024,128]{1,0:T(8,128)(2,1)} %b_any.1, bf16[1024,128]{1,0:T(8,128)(2,1)} %c_any.1, ...), custom_call_target="tpu_custom_call" | custom-call | tf_op jit(solution)/shard_map/pallas_call | solution.py:519
  53.0 2.2 %shard_map.102 = (bf16[1024,1024]{1,0:T(8,128)(2,1)}, bf16[1024,1024]{1,0:T(8,128)(2,1)}, f32[16,1024]{1,0:T(8,128)}, f32[128,128]{1,0:T(8,128)}, f32[128,128]{1,0:T(8,128)}) custom-call(bf16[1024,1024]{1,0:T(8,128)(2,1)S(1)} %get-tuple-element.10.refs_0_, bf16[1024,1024]{1,0:T(8,128)(2,1)S(1)} %get-tuple-element.11.refs_1_, ...), custom_call_target="tpu_custom_call" | custom-call | tf_op jit(solution)/shard_map/pallas_call | solution.py:469

commit v5 on v4

--- a/solution.py
+++ b/solution.py
@@ -307,19 +307,15 @@
     pair_f = pair_send(0, th.at[other], pf, piece_of)
     whole_load(1).wait()
     a_exp[...] = nn(by_chunk(parts_a), spread[...])
-    for c in reversed(range(nc // 2, nc)):
-        bwd_local(c)
-    send_lam.wait_recv()
-    go_f = combine(0, pair_f, th, pf, cmf, rf, True)
-    for c in reversed(range(nc // 2)):
+    for c in reversed(range(nc)):
         bwd_local(c)
     to_halves(grad, tb)
     pair_b = pair_send(1, tb.at[other], pb, piece_of)
     whole_load(3).wait()
-    for c in range(nc // 4):
-        inner(c)
+    send_lam.wait_recv()
+    go_f = combine(0, pair_f, th, pf, cmf, rf, True)
     go_b = combine(1, pair_b, tb, pb, cmb, rb, False)
-    for c in range(nc // 4, nc // 2):
+    for c in range(nc // 2):
         inner(c)
     ret_f = scan_pieces(go_f, 2, rf, esf, ref_, range(chips))
     for c in range(nc // 2, 3 * nc // 4):
@@ -390,13 +386,12 @@
         c = near(i)
         dbs[c] += nt(xs[c], tp[c])
 
+    send_2b = hand_out(3, ret_b, reb, tb, pb, p2b, peb, grad, False)
     for i in range(3):
         dc_chunk(i)
     rs_poll(0, dcs, 0)
-    send_2b = hand_out(3, ret_b, reb, tb, pb, p2b, peb, grad, False)
-    for i in range(3, nc):
+    for i in range(3, min(5, nc)):
         dc_chunk(i)
-    rs_poll(0, dcs, 1)
     take_in(send_2b, peb, grad)
 
     for c in reversed(range(nc)):
@@ -409,9 +404,11 @@
     for i in range(3):
         db_chunk(i)
     rs_poll(1, dbs, 0)
-    rs_poll(0, dcs, 2) if far > 2 else None
+    for i in range(5, nc):
+        dc_chunk(i)
     for i in range(3, nc):
         db_chunk(i)
+    rs_poll(0, dcs, 1)
 
     last_row = iota((q, width), 0) == q - 1
 
@@ -436,9 +433,9 @@
         for c in range(done, upto):
             outputs(c)
         done = upto
-        if 2 < step + 2 < far:
-            rs_poll(0, dcs, step + 2)
         rs_poll(1, dbs, step)
+        if step + 1 < far:
+            rs_poll(0, dcs, step + 1)
     for c in range(done, nc):
         outputs(c)
     rs_end(0, dcs, gc_ref)

time: 55.4 us -> 52.9 us (0.955)
  Pallas kernels: 54.6 us -> 52 us
    pallas_call x1, Pallas kernels: 52.3 us -> 49.8 us  [body(): pl.pallas_call(functools.partial(kernel, chips, ring), out_shape=(vm((len...]
where the time goes in v5:
time: 52.9 us; the launch traced here: 52.8 us
  Pallas kernels  52 us (98%)
  between operations  0.8 us (2%)
    pallas_call x1, Pallas kernels, body(): pl.pallas_call(functools.partial(kernel, chips, ring), out_shape=(vm((len...  49.8 us
    pallas_call x1, Pallas kernels, finish(): pl.pallas_call(finish_kernel, out_shape=tuple((jax.ShapeDtypeStruct(a.sha...  2.23 us

profile of v5, /device:TPU:8, one launch (start us, length us, event | category | flops | bytes accessed | tf_op | source)
XLA Modules:
  0.0 52.8 jit_solution(1194890787723967923)
XLA Ops:
  0.6 49.8 %shard_map.101 = (bf16[1024,1024]{1,0:T(8,128)(2,1)S(1)}, bf16[1024,1024]{1,0:T(8,128)(2,1)S(1)}, f32[16,1024]{1,0:T(8,128)S(1)}, f32[128,128]{1,0:T(8,128)S(1)}, f32[128,128]{1,0:T(8,128)S(1)}) custom-call(bf16[1024,1024]{1,0:T(8,128)(2,1)} %x_ref.1, f32[16,1024]{1,0:T(8,128)} %ld_any.1, bf16[1024,128]{1,0:T(8,128)(2,1)} %b_any.1, bf16[1024,128]{1,0:T(8,128)(2,1)} %c_any.1, ...), custom_call_target="tpu_custom_call" | custom-call | tf_op jit(solution)/shard_map/pallas_call | solution.py:516
  50.4 2.2 %shard_map.102 = (bf16[1024,1024]{1,0:T(8,128)(2,1)}, bf16[1024,1024]{1,0:T(8,128)(2,1)}, f32[16,1024]{1,0:T(8,128)}, f32[128,128]{1,0:T(8,128)}, f32[128,128]{1,0:T(8,128)}) custom-call(bf16[1024,1024]{1,0:T(8,128)(2,1)S(1)} %get-tuple-element.10.refs_0_, bf16[1024,1024]{1,0:T(8,128)(2,1)S(1)} %get-tuple-element.11.refs_1_, ...), custom_call_target="tpu_custom_call" | custom-call | tf_op jit(solution)/shard_map/pallas_call | solution.py:466

commit v6 on v5

--- a/solution.py
+++ b/solution.py
@@ -49,7 +49,7 @@
            xs, ds, a_exp, inv_exp, gmat, hmat, sp, tp, mm, mt, dcs, dbs, bnd,
            spread, parts_a, parts_i, rows, heads_of, tri_s, skipe,
            state, grad, th, tb, lamh, lamp, pf, pb, cmf, cmb, rf, rb, esf, esb,
-           ref_, reb, p2f, p2b, pef, peb, rsbuf,
+           ref_, reb, p2f, p2b, pef, peb, rsbuf, rsout,
            in_s, lam_s, lam_r, pair_s, pair_r, a2a_s, a2a_r, rs_s, rs_r):
     seq = lax.axis_index("seq")
     z = lax.axis_index("exp")
@@ -118,10 +118,10 @@
     pl.semaphore_signal(barrier, inc=1, device_id=partner, device_id_type=MESH)
     for d in range(count):
         pl.semaphore_signal(barrier, inc=1, device_id=chip_dev(chip_to(d)), device_id_type=MESH)
-    z_dn = lax.rem(z + ring - 1, ring)
-    z_up = lax.rem(z + 1, ring)
-    pl.semaphore_signal(barrier, inc=1, device_id=(seq, z_dn), device_id_type=MESH)
-    pl.semaphore_signal(barrier, inc=1, device_id=(seq, z_up), device_id_type=MESH)
+    relay = far // 2
+    for hop in range(1, relay + 1):
+        for to in (lax.rem(z + hop, ring), lax.rem(z + ring - hop, ring)):
+            pl.semaphore_signal(barrier, inc=1, device_id=(seq, to), device_id_type=MESH)
 
     def head_of(shape, axis):
         return lax.shift_right_logical(iota(shape, axis), HEAD.bit_length() - 1)
@@ -301,7 +301,7 @@
     for c in range(nc):
         fwd_local(c)
     to_halves(state, th)
-    pl.semaphore_wait(barrier, chips + 2)
+    pl.semaphore_wait(barrier, chips + 2 * relay)
     send_lam = remote(lamh.at[other], lamp, lam_s, lam_r, partner)
     send_lam.start()
     pair_f = pair_send(0, th.at[other], pf, piece_of)
@@ -341,42 +341,55 @@
     hq = q // 2
     started = {}
 
-    def chunk_at(way, step):
-        gap = far - step
+    def away(way, gap):
         return lax.rem(z + (ring - gap if way == 0 else gap), ring)
 
-    def rs_send(t, own, way, step, long):
-        lo = (way if long else 1 - way) * hq
-        first_step = 0 if long else 1
-        k = chunk_at(way, step)
-        if step == first_step:
-            src = own.at[k, pl.ds(lo, hq)]
-        else:
-            started[t, way, step - 1, long].wait_recv()
-            rsbuf[t, way, step - 1, lo:lo + hq, :] += own[k, lo:lo + hq, :]
-            src = rsbuf.at[t, way, step - 1, pl.ds(lo, hq)]
-        copy = remote(src, rsbuf.at[t, way, step, pl.ds(lo, hq)],
-                      rs_s.at[t, way, step, int(long)], rs_r.at[t, way, step, int(long)],
-                      (seq, z_dn if way == 0 else z_up))
+    def rows_at(way, gap):
+        return pl.ds(way * hq, hq) if gap == far else pl.ds(0, q)
+
+    def rs_send(t, way, gap, src):
+        hop = gap - relay if gap > relay else gap
+        span = rows_at(way, gap)
+        copy = remote(src.at[span], rsbuf.at[t, way, gap - 1, span],
+                      rs_s.at[t, way, gap - 1], rs_r.at[t, way, gap - 1], (seq, away(way, hop)))
         copy.start()
-        started[t, way, step, long] = copy
-
-    def rs_poll(t, own, step):
+        started[t, way, gap] = copy
+
+    def rs_first(t, own, gaps):
+        for gap in gaps:
+            for way in range(2):
+                rs_send(t, way, gap, own.at[away(way, gap)])
+
+    def rs_second(t, own):
         for way in range(2):
-            rs_send(t, own, way, step, True)
-        if step + 1 < far:
+            for gap in range(relay + 1, far + 1):
+                started[t, way, gap].wait_recv()
+            k = away(way, relay)
+            for side in range(2):
+                span = slice(side * hq, (side + 1) * hq)
+                value = own[k, span, :]
+                for gap in range(relay + 1, far + 1):
+                    if gap < far or side == way:
+                        value = value + rsbuf[t, way, gap - 1, span, :]
+                rsout[t, way, span, :] = value
+            rs_send(t, way, relay, rsout.at[t, way])
+
+    def rs_end(t, own, out):
+        value = own[z]
+        for gap in range(1, relay + 1):
             for way in range(2):
-                rs_send(t, own, way, step + 1, False)
-
-    def rs_end(t, own, out):
-        for way in range(2):
-            for long in (False, True):
-                started[t, way, far - 1, long].wait_recv()
-        out[...] = own[z] + rsbuf[t, 0, far - 1] + rsbuf[t, 1, far - 1]
+                started[t, way, gap].wait_recv()
+                value = value + rsbuf[t, way, gap - 1]
+        out[...] = value
+
+    far_gaps = list(range(far, relay, -1))
+    near_gaps = list(range(1, relay))
+    order = [(0, far)] + [(way, g) for g in far_gaps[1:] + near_gaps + [relay] for way in range(2)]
+    n_far = 1 + 2 * (len(far_gaps) - 1)
+    n_first = n_far + 2 * len(near_gaps)
 
     def near(i):
-        gap = far - (i + 1) // 2
-        return lax.rem(z + (gap if i % 2 == 1 else ring - gap), ring)
+        return away(*order[i]) if i < len(order) else z
 
     def dc_chunk(i):
         c = near(i)
@@ -387,11 +400,12 @@
         dbs[c] += nt(xs[c], tp[c])
 
     send_2b = hand_out(3, ret_b, reb, tb, pb, p2b, peb, grad, False)
-    for i in range(3):
+    for i in range(n_far):
         dc_chunk(i)
-    rs_poll(0, dcs, 0)
-    for i in range(3, min(5, nc)):
+    rs_first(0, dcs, far_gaps)
+    for i in range(n_far, n_first):
         dc_chunk(i)
+    rs_first(0, dcs, near_gaps)
     take_in(send_2b, peb, grad)
 
     for c in reversed(range(nc)):
@@ -401,14 +415,16 @@
         bnd[c:c + 1, :] = jnp.sum(low.astype(F32) * gmat[c], axis=0, keepdims=True)
         if c:
             grad[...] = rows[c:c + 1, :] * (later + hmat[c])
-    for i in range(3):
+    for i in range(n_far):
         db_chunk(i)
-    rs_poll(1, dbs, 0)
-    for i in range(5, nc):
+    rs_first(1, dbs, far_gaps)
+    for i in range(n_far, n_first):
+        db_chunk(i)
+    rs_first(1, dbs, near_gaps)
+    for i in range(n_first, nc):
         dc_chunk(i)
-    for i in range(3, nc):
+    for i in range(n_first, nc):
         db_chunk(i)
-    rs_poll(0, dcs, 1)
 
     last_row = iota((q, width), 0) == q - 1
 
@@ -427,17 +443,12 @@
         per_head = nn(pieces(diff, 2, 1), heads_of[...])
         gld_ref[:, rc] = tn(pieces(per_head, 3, 0), tri_s[...])
 
-    done = 0
-    for step in range(1, far):
-        upto = nc * step // far
-        for c in range(done, upto):
-            outputs(c)
-        done = upto
-        rs_poll(1, dbs, step)
-        if step + 1 < far:
-            rs_poll(0, dcs, step + 1)
-    for c in range(done, nc):
+    for c in range(nc):
         outputs(c)
+        if c == nc // 4 - 1:
+            rs_second(0, dcs)
+        if c == 3 * nc // 4 - 1:
+            rs_second(1, dbs)
     rs_end(0, dcs, gc_ref)
     rs_end(1, dbs, gb_ref)
     for copy in [send_lam, *pair_f, *pair_b, *go_f, *go_b, *ret_f, *ret_b,
@@ -504,12 +515,12 @@
         vm(msg, F32), vm(msg, F32),
         vm(msg_l, F32), vm(msg, F32), vm(msg_l, F32), vm(msg, F32), vm(msg, F32), vm(msg, F32),
         vm(msg, F32), vm(msg, F32), vm(msg, F32), vm(msg, F32), vm(msg, F32), vm(msg, F32),
-        vm((2, 2, far, q, state_n), F32),
+        vm((2, 2, far, q, state_n), F32), vm((2, 2, q, state_n), F32),
         pltpu.SemaphoreType.DMA((2, 6)),
         pltpu.SemaphoreType.DMA, pltpu.SemaphoreType.DMA,
         pltpu.SemaphoreType.DMA((4, chips)), pltpu.SemaphoreType.DMA((4, chips)),
         pltpu.SemaphoreType.DMA((4, chips)), pltpu.SemaphoreType.DMA((4, chips)),
-        pltpu.SemaphoreType.DMA((2, 2, far, 2)), pltpu.SemaphoreType.DMA((2, 2, far, 2)),
+        pltpu.SemaphoreType.DMA((2, 2, far)), pltpu.SemaphoreType.DMA((2, 2, far)),
     ]
     whole = pl.BlockSpec(memory_space=pltpu.VMEM)
     outside = pl.BlockSpec(memory_space=pltpu.HBM)

time: 52.9 us -> 54 us (1.021)
  the two profiles are of different devices: /device:TPU:8 before, /device:TPU:1 now
where the time goes in v6:
time: 54 us; the launch traced here: 53.9 us
  Pallas kernels  53.1 us (98%)
  between operations  0.8 us (1%)
    pallas_call x1, Pallas kernels, body(): pl.pallas_call(functools.partial(kernel, chips, ring), out_shape=(vm((len...  50.9 us
    pallas_call x1, Pallas kernels, finish(): pl.pallas_call(finish_kernel, out_shape=tuple((jax.ShapeDtypeStruct(a.sha...  2.23 us

profile of v6, /device:TPU:1, one launch (start us, length us, event | category | flops | bytes accessed | tf_op | source)
XLA Modules:
  0.0 53.9 jit_solution(7176241392567992816)
XLA Ops:
  0.6 50.9 %shard_map.101 = (bf16[1024,1024]{1,0:T(8,128)(2,1)S(1)}, bf16[1024,1024]{1,0:T(8,128)(2,1)S(1)}, f32[16,1024]{1,0:T(8,128)S(1)}, f32[128,128]{1,0:T(8,128)S(1)}, f32[128,128]{1,0:T(8,128)S(1)}) custom-call(bf16[1024,1024]{1,0:T(8,128)(2,1)} %x_ref.1, f32[16,1024]{1,0:T(8,128)} %ld_any.1, bf16[1024,128]{1,0:T(8,128)(2,1)} %b_any.1, bf16[1024,128]{1,0:T(8,128)(2,1)} %c_any.1, ...), custom_call_target="tpu_custom_call" | custom-call | tf_op jit(solution)/shard_map/pallas_call | solution.py:527
  51.5 2.2 %shard_map.102 = (bf16[1024,1024]{1,0:T(8,128)(2,1)}, bf16[1024,1024]{1,0:T(8,128)(2,1)}, f32[16,1024]{1,0:T(8,128)}, f32[128,128]{1,0:T(8,128)}, f32[128,128]{1,0:T(8,128)}) custom-call(bf16[1024,1024]{1,0:T(8,128)(2,1)S(1)} %get-tuple-element.10.refs_0_, bf16[1024,1024]{1,0:T(8,128)(2,1)S(1)} %get-tuple-element.11.refs_1_, ...), custom_call_target="tpu_custom_call" | custom-call | tf_op jit(solution)/shard_map/pallas_call | solution.py:477

commit v7 on v5

--- a/solution.py
+++ b/solution.py
@@ -204,7 +204,8 @@
         return out
 
     def pass_on(base, d, src, dst, p):
-        copy = remote(src.at[p], dst.at[chip], a2a_s.at[base, d], a2a_r.at[base, d], chip_dev(p))
+        span = pl.ds(0, lb * pr + (lb if base == 0 else 0))
+        copy = remote(src.at[p, span], dst.at[chip, span], a2a_s.at[base, d], a2a_r.at[base, d], chip_dev(p))
         copy.start()
         return copy
 

time: 52.9 us -> 52.6 us (level)
  no operation moved by 1% of the time
where the time goes in v7:
time: 52.6 us; the launch traced here: 52.5 us
  Pallas kernels  51.7 us (98%)
  between operations  0.8 us (2%)
    pallas_call x1, Pallas kernels, body(): pl.pallas_call(functools.partial(kernel, chips, ring), out_shape=(vm((len...  49.5 us
    pallas_call x1, Pallas kernels, finish(): pl.pallas_call(finish_kernel, out_shape=tuple((jax.ShapeDtypeStruct(a.sha...  2.23 us

profile of v7, /device:TPU:8, one launch (start us, length us, event | category | flops | bytes accessed | tf_op | source)
XLA Modules:
  0.0 52.5 jit_solution(14732895884226255562)
XLA Ops:
  0.6 49.5 %shard_map.101 = (bf16[1024,1024]{1,0:T(8,128)(2,1)S(1)}, bf16[1024,1024]{1,0:T(8,128)(2,1)S(1)}, f32[16,1024]{1,0:T(8,128)S(1)}, f32[128,128]{1,0:T(8,128)S(1)}, f32[128,128]{1,0:T(8,128)S(1)}) custom-call(bf16[1024,1024]{1,0:T(8,128)(2,1)} %x_ref.1, f32[16,1024]{1,0:T(8,128)} %ld_any.1, bf16[1024,128]{1,0:T(8,128)(2,1)} %b_any.1, bf16[1024,128]{1,0:T(8,128)(2,1)} %c_any.1, ...), custom_call_target="tpu_custom_call" | custom-call | tf_op jit(solution)/shard_map/pallas_call | solution.py:517
  50.1 2.2 %shard_map.102 = (bf16[1024,1024]{1,0:T(8,128)(2,1)}, bf16[1024,1024]{1,0:T(8,128)(2,1)}, f32[16,1024]{1,0:T(8,128)}, f32[128,128]{1,0:T(8,128)}, f32[128,128]{1,0:T(8,128)}) custom-call(bf16[1024,1024]{1,0:T(8,128)(2,1)S(1)} %get-tuple-element.10.refs_0_, bf16[1024,1024]{1,0:T(8,128)(2,1)S(1)} %get-tuple-element.11.refs_1_, ...), custom_call_target="tpu_custom_call" | custom-call | tf_op jit(solution)/shard_map/pallas_call | solution.py:467
